TPU v7x, 32 devices: a whole 2x2x4 slice. The times are simulated.
32 devices in a mesh: fsdp: 8 (over y, x, core), tensor: 4 (over z).
Axes of the slice: x: 2, y: 2, z: 4, core: 2. Of those that a mesh axis runs over, the one named last changes fastest.
Arguments:
- tokens: bfloat16 [8192, 1536], P(('fsdp', 'tensor')), may hold values from -6 to 6
- w_query: bfloat16 [1536, 1536], P('fsdp', 'tensor'), may hold values from -0.15625 to 0.15625
- key_weight_matrix: bfloat16 [1536, 768], P('fsdp', 'tensor'), may hold values from -0.15625 to 0.15625
- value_weight_matrix: bfloat16 [1536, 768], P('fsdp', 'tensor'), may hold values from -0.15625 to 0.15625
- w_out: bfloat16 [1536, 1536], P('tensor', 'fsdp'), may hold values from -6 to 6
- w_gate: bfloat16 [1536, 4096], P('fsdp', 'tensor'), may hold values from -0.15625 to 0.15625
- w_up: bfloat16 [1536, 4096], P('fsdp', 'tensor'), may hold values from -0.15625 to 0.15625
- w_down: bfloat16 [4096, 1536], P('tensor', 'fsdp'), may hold values from -0.1875 to 0.1875
- norm_attn: bfloat16 [1536], P('fsdp'), may hold values from 0.5 to 1.5
- norm_ffn: bfloat16 [1536], P('fsdp'), may hold values from 0.5 to 1.5
- grad_out: bfloat16 [8192, 1536], P(('fsdp', 'tensor')), may hold values from -6 to 6
Outputs:
- layer_out: bfloat16 [8192, 1536], P(('fsdp', 'tensor'))
- grad_tokens: bfloat16 [8192, 1536], P(('fsdp', 'tensor'))
- grad_query: float32 [1536, 1536], P('fsdp', 'tensor')
- grad_key: float32 [1536, 768], P('fsdp', 'tensor')
- grad_value: float32 [1536, 768], P('fsdp', 'tensor')
- grad_outproj: float32 [1536, 1536], P('tensor', 'fsdp')
- grad_gate: float32 [1536, 4096], P('fsdp', 'tensor')
- grad_upproj: float32 [1536, 4096], P('fsdp', 'tensor')
- grad_down: float32 [4096, 1536], P('tensor', 'fsdp')
- grad_norm_attn: float32 [1536], P('fsdp')
- grad_norm_ffn: float32 [1536], P('fsdp')
- rms_stats: float32 [3], replicated
All inputs are finite; a program needn't handle non-finite values.
Results may differ from a plain program's by a relative error of at most 0.024.
Values may be sent and summed in bfloat16 or wider, within the bound.
No kernel may reach another device: no remote copies, remote signals or barrier semaphores. Data moves between devices by JAX's collectives and lax.ppermute only.
A program may use at most 192 MiB of HBM per device.

v0:
```python
import functools
import jax
import jax.numpy as jnp
from jax import lax
from jax.experimental import pallas as pl
from jax.experimental.pallas import tpu as pltpu
from jax.sharding import Mesh, PartitionSpec as P

HEAD = 96
LANES = 128
SEQUENCE_LENGTH = 4096
SPANS = 4
EPSILON = 1e-05
ROPE_BASE = 100000.0
MASKED = -1e30
LOG2E = 1.4426950408889634
NT = (((1,), (1,)), ((), ()))
NN = (((1,), (0,)), ((), ()))
TN = (((0,), (0,)), ((), ()))
F32 = jnp.float32
BF16 = jnp.bfloat16


def mm(left, right, dims):
    return lax.dot_general(left, right, dims, preferred_element_type=F32)


def widen(piece):
    return jnp.concatenate([piece, jnp.zeros((piece.shape[0], LANES - HEAD), piece.dtype)], axis=1)


def swapped(value):
    half = HEAD // 2
    return jnp.concatenate([value[:, half:HEAD], value[:, :half]], axis=1)


def rotary(tables, place):
    cos_in, sin_in, cos_out, sin_out = tables
    at = pl.ds(place, 1)
    cosine = cos_out[at, :] * cos_in[...] - sin_out[at, :] * sin_in[...]
    return cosine, sin_out[at, :] * cos_in[...] + cos_out[at, :] * sin_in[...]


def attend_kernel(ids, own, other, out, q_s, kv_s, o_s, lse_s, acc_s, vt_s, *, block, tile):
    z, t = ids[0], ids[1]
    c = lax.rem(t, 2)
    spans = 4
    rows_all = q_s.shape[0]
    for zj in range(4):
        for r in range(spans):
            at = pl.multiple_of(((t ^ r) * spans + zj) * block, block)
            at_other = pl.multiple_of(((t ^ 1 ^ r) * spans + zj) * block, block)
            q_s[pl.ds(at, block), :] = widen(own[zj, :, r * HEAD : (r + 1) * HEAD])
            kv_s[c, pl.ds(at, block), :] = widen(own[zj, :, (spans + r) * HEAD : (spans + r + 1) * HEAD])
            kv_s[1 - c, pl.ds(at_other, block), :] = widen(other[zj, :, r * HEAD : (r + 1) * HEAD])
    factor = HEAD ** (-0.5) * LOG2E
    is_count = lax.broadcasted_iota(jnp.int32, (tile, LANES), 1) == HEAD

    def values(i, _):
        rows = pl.ds(pl.multiple_of(i * tile, tile), tile)
        vals = kv_s[1, rows, :]
        vt_s[:, rows] = jnp.transpose(jnp.where(is_count, jnp.ones_like(vals), vals))
        return 0

    lax.fori_loop(0, rows_all // tile, values, 0)

    def step(query, j, before, mask):
        rows = pl.ds(pl.multiple_of(j * tile, tile), tile)
        scores = mm(kv_s[0, rows, :], query, NT) * factor
        if mask is not None:
            scores = jnp.where(mask, scores, MASKED)
        top = jnp.maximum(before, jnp.max(scores, axis=0, keepdims=True))
        expo = jnp.exp2(scores - top).astype(BF16)
        acc_s[...] = acc_s[...] * jnp.exp2(before - top) + mm(vt_s[:, rows], expo, NN)
        return top

    def row_block(i, _):
        at = pl.multiple_of(i * tile, tile)
        query = q_s[pl.ds(at, tile), :]
        acc_s[...] = jnp.zeros_like(acc_s)
        top = lax.fori_loop(0, i, lambda j, top: step(query, j, top, None), jnp.full((1, tile), MASKED, F32))
        mask = lax.broadcasted_iota(jnp.int32, (tile, tile), 0) <= lax.broadcasted_iota(jnp.int32, (tile, tile), 1)
        top = step(query, i, top, mask)
        acc = acc_s[...]
        denom = acc[HEAD : HEAD + 1, :]
        o_s[pl.ds(at, tile), :] = jnp.transpose(acc / denom).astype(BF16)
        lse_s[:, pl.ds(at, tile)] = jnp.broadcast_to(top + jnp.log2(denom), (8, tile))
        return 0

    lax.fori_loop(0, rows_all // tile, row_block, 0)
    for zj in range(4):
        for r in range(spans):
            at = pl.multiple_of(((t ^ r) * spans + zj) * block, block)
            out[zj, :, r * HEAD : (r + 1) * HEAD] = o_s[pl.ds(at, block), :HEAD]


VM = pl.BlockSpec(memory_space=pltpu.VMEM)
SM = pl.BlockSpec(memory_space=pltpu.SMEM)


def shape(dims, dtype=BF16):
    return jax.ShapeDtypeStruct(dims, dtype)


def params(room):
    return pltpu.CompilerParams(vmem_limit_bytes=room * 1024 * 1024)


def attend(ids, own, other, tile=1024):
    block = own.shape[1]
    rows = block * 16
    return pl.pallas_call(
        functools.partial(attend_kernel, block=block, tile=tile),
        out_shape=[shape((4, block, 4 * HEAD)), shape((rows, LANES)), shape((2, rows, LANES)), shape((rows, LANES)), shape((8, rows), F32)],
        in_specs=[SM] + [VM] * 2,
        out_specs=[VM] * 5,
        scratch_shapes=[pltpu.VMEM((LANES, tile), F32), pltpu.VMEM((LANES, rows), BF16)],
        compiler_params=params(22),
        cost_estimate=pl.CostEstimate(flops=int(21e9), bytes_accessed=1, transcendentals=0),
        name="attend",
    )(ids, own, other)


def attend_back_kernel(ids, q_s, kv_s, o_s, lse_s, cos_in, sin_in, cos_out, sin_out, g, dq_out, keep_out, give_out, g_s, qx_s, kx_s, delta_s, dq_s, dk_s, dv_s, *, block, tile):
    z, t = ids[0], ids[1]
    spans = 4
    rows_all = q_s.shape[0]
    tiles = rows_all // tile
    for zj in range(4):
        for r in range(spans):
            at = pl.multiple_of(((t ^ r) * spans + zj) * block, block)
            g_s[pl.ds(at, block), :] = widen(g[zj, :, r * HEAD : (r + 1) * HEAD])

    def prepare(i, _):
        at = pl.multiple_of(i * tile, tile)
        rows = pl.ds(at, tile)
        query = q_s[rows, :]
        keys = kv_s[0, rows, :]
        qx_s[rows, :LANES] = query
        qx_s[rows, LANES:] = widen(swapped(query))
        kx_s[rows, :LANES] = keys
        kx_s[rows, LANES:] = widen(swapped(keys))
        both = g_s[rows, :].astype(F32) * o_s[rows, :].astype(F32)
        delta = jnp.sum(both, axis=1, keepdims=True)
        delta_s[:, rows] = jnp.transpose(jnp.broadcast_to(delta, (tile, LANES)))[:8]
        dq_s[rows, :] = jnp.zeros((tile, 2 * LANES), F32)
        return 0

    lax.fori_loop(0, tiles, prepare, 0)
    factor = HEAD ** (-0.5) * LOG2E
    scale = HEAD ** (-0.5)

    def step(i, keys, vals, kx, mask):
        rows = pl.ds(pl.multiple_of(i * tile, tile), tile)
        query = qx_s[rows, :]
        grad = g_s[rows, :]
        scores = mm(keys, query[:, :LANES], NT) * factor - lse_s[:1, rows]
        if mask is not None:
            scores = jnp.where(mask, scores, MASKED)
        prob = jnp.exp2(scores)
        through = mm(vals, grad, NT)
        ds = (prob * (through - delta_s[:1, rows])).astype(BF16)
        dv_s[...] += mm(prob.astype(BF16), grad, NN)
        dk_s[...] += mm(ds, query, NN)
        dq_s[rows, :] += mm(ds, kx, TN)

    def column_block(j, _):
        rows = pl.ds(pl.multiple_of(j * tile, tile), tile)
        kx = kx_s[rows, :]
        keys = kx[:, :LANES]
        vals = kv_s[1, rows, :]
        dk_s[...] = jnp.zeros_like(dk_s)
        dv_s[...] = jnp.zeros_like(dv_s)
        mask = lax.broadcasted_iota(jnp.int32, (tile, tile), 0) <= lax.broadcasted_iota(jnp.int32, (tile, tile), 1)
        step(j, keys, vals, kx, mask)
        lax.fori_loop(j + 1, tiles, lambda i, _: (step(i, keys, vals, kx, None), 0)[1], 0)
        dk = dk_s[...] * scale
        turns = [rotary((cos_in, sin_in, cos_out, sin_out), j * (tile // block) + b) for b in range(tile // block)]
        cosine, sine = (jnp.concatenate(parts, axis=0) for parts in zip(*turns))
        dk = dk[:, :LANES] * cosine - dk[:, LANES:] * sine
        dv = dv_s[...]
        first = lax.rem(t, 2) == 0
        keep_out[rows, :] = jnp.where(first, dk, dv).astype(BF16)
        give_out[rows, :] = jnp.where(first, dv, dk).astype(BF16)
        return 0

    lax.fori_loop(0, tiles, column_block, 0)
    for zj in range(4):
        for r in range(spans):
            rows = pl.ds(pl.multiple_of(((t ^ r) * spans + zj) * block, block), block)
            cosine, sine = rotary((cos_in, sin_in, cos_out, sin_out), (t ^ r) * spans + zj)
            dq = dq_s[rows, :] * scale
            dq_out[zj, :, r * HEAD : (r + 1) * HEAD] = (
                dq[:, :LANES] * cosine - dq[:, LANES:] * sine
            ).astype(BF16)[:, :HEAD]


def attend_back(ids, q, kv, o, lse, tables, grads, tile=1024):
    block = grads.shape[1]
    rows = block * 16
    return pl.pallas_call(
        functools.partial(attend_back_kernel, block=block, tile=tile),
        out_shape=[shape((4, block, 4 * HEAD))] + [shape((rows, LANES))] * 2,
        in_specs=[SM] + [VM] * 9,
        out_specs=[VM] * 3,
        scratch_shapes=[
            pltpu.VMEM((rows, LANES), BF16),
            pltpu.VMEM((rows, 2 * LANES), BF16),
            pltpu.VMEM((rows, 2 * LANES), BF16),
            pltpu.VMEM((8, rows), F32),
            pltpu.VMEM((rows, 2 * LANES), F32),
            pltpu.VMEM((tile, 2 * LANES), F32),
            pltpu.VMEM((tile, LANES), F32),
        ],
        compiler_params=params(36),
        cost_estimate=pl.CostEstimate(flops=int(39e9), bytes_accessed=1, transcendentals=0),
        name="attend_back",
    )(ids, q, kv, o, lse, *tables, grads)


def offsets(ids, count, part):
    if count == 1:
        return [0]
    return [pl.multiple_of(ids[2] * part, LANES), pl.multiple_of((1 - ids[2]) * part, LANES)]


def call(kernel, outs, name, scratch=(), micros=0, room=14):
    def run(ids, *args):
        return pl.pallas_call(
            kernel,
            out_shape=[shape(*o) if isinstance(o[0], tuple) else shape(o) for o in outs],
            in_specs=[SM] + [VM] * len(args),
            out_specs=[VM] * len(outs),
            scratch_shapes=[pltpu.VMEM(*item) for item in scratch],
            compiler_params=params(room),
            cost_estimate=pl.CostEstimate(flops=int(micros * 1e9) + 1, bytes_accessed=1, transcendentals=0),
            name=name,
        )(ids, *args)

    return run


def split(refs, *counts):
    refs = list(refs)
    groups = []
    for count in counts:
        groups.append(refs[:count])
        refs = refs[count:]
    return groups


def prepare_attn(ids, w_query, w_key, w_value, w_out, gain):
    shard = w_query.shape[0]

    def kernel(ids, query, key, value, out, gain, *refs):
        pieces, made = split(refs, SPANS, 1)
        made = made[0]
        scale = gain[...]

        def turned(ref, at):
            return jnp.transpose(ref[:, at * HEAD : (at + 1) * HEAD].astype(F32) * scale).astype(BF16)

        for place in range(SPANS):
            made[place, :HEAD] = turned(query, place)
            made[place, HEAD : 2 * HEAD] = turned(value if place % 2 else key, place // 2)
            made[place, 2 * HEAD :] = jnp.transpose(out[:, place * HEAD : (place + 1) * HEAD].astype(F32)).astype(BF16)
        for r in range(SPANS):
            pieces[r][...] = made[ids[1] ^ r]

    scratch = [((SPANS, 3 * HEAD, shard), BF16)]
    return call(kernel, [(3 * HEAD, shard)] * SPANS, "prepare_attn", scratch)(
        ids, w_query, w_key, w_value, w_out.T, gain
    )


def prepare_ffn(ids, w_gate, w_up, w_down, gain):
    shard = w_gate.shape[0]
    units = w_gate.shape[1] // SPANS

    def kernel(ids, gate, up, down, gain, *pieces):
        scale = gain[...]
        for r in range(SPANS):
            at = pl.multiple_of((ids[1] ^ r) * units, LANES)
            pieces[r][0] = (gate[:, pl.ds(at, units)].astype(F32) * scale).astype(BF16)
            pieces[r][1] = (up[:, pl.ds(at, units)].astype(F32) * scale).astype(BF16)
            pieces[r][2] = down[:, pl.ds(at, units)]

    return call(kernel, [(3, shard, units)] * SPANS, "prepare_ffn")(ids, w_gate, w_up, w_down.T, gain)


def join_attn(ids, pieces):
    rows, shard = pieces[0].shape

    def kernel(ids, *refs):
        pieces, (out,), (made,) = split(refs, SPANS, 1, 1)
        for r, piece in enumerate(pieces):
            made[ids[1] ^ r] = piece[...]
        for place in range(SPANS):
            out[:, place * shard : (place + 1) * shard] = made[place]

    return call(kernel, [(rows, SPANS * shard)], "join_attn", [((SPANS, rows, shard), BF16)])(ids, *pieces)[0]


def join_ffn(ids, pieces):
    _, shard, units = pieces[0].shape

    def kernel(ids, *refs):
        pieces, (out,) = split(refs, SPANS, 1)
        for r, piece in enumerate(pieces):
            out[:, pl.ds(pl.multiple_of((ids[1] ^ r) * shard, 16), shard), :] = piece[...]

    return call(kernel, [(3, SPANS * shard, units)], "join_ffn")(ids, *pieces)[0]


def part_attn(ids, own, one, three):
    rows, part = own.shape
    shard = part // SPANS

    def kernel(ids, own, one, three, *refs):
        pieces, (made,) = split(refs, SPANS, 1)
        total = (own[...].astype(F32) + one[...].astype(F32) + three[...].astype(F32)).astype(BF16)
        for place in range(SPANS):
            made[place] = total[:, place * shard : (place + 1) * shard]
        for r, piece in enumerate(pieces):
            piece[...] = made[ids[1] ^ r]

    return call(kernel, [(rows, shard)] * SPANS, "part_attn", [((SPANS, rows, shard), BF16)])(ids, own, one, three)


def distinct(items):
    arrays = list({id(item[0]): item[0] for item in items}.values())
    index = {id(array): i for i, array in enumerate(arrays)}

    def rows_of(refs, item, rows):
        return refs[index[id(item[0])]][(*item[1], rows)]

    return arrays, rows_of


def project(ids, x, weights, tables):
    block = x[0].shape[0]
    parts = len(weights[0])
    part = weights[0][0][0].shape[-1]
    arrays, rows_of = distinct([item for items in weights for item in items])
    first = slice(0, 2 * HEAD)

    def kernel(ids, *refs):
        xs, ws, tables, (out,) = split(refs, SPANS, len(arrays), 4, 1)
        z, t = ids[0], ids[1]
        at = offsets(ids, parts, part)
        is_value = lax.rem(t, 2) == 1
        for r, x in enumerate(xs):
            cosine, sine = rotary(tables, (t ^ r) * SPANS + z)
            cosine, sine = cosine[:, :HEAD], sine[:, :HEAD]
            cos_kv = jnp.where(is_value, 1.0, cosine)
            sin_kv = jnp.where(is_value, 0.0, sine)
            for k in range(4):
                made = sum(mm(x[:, pl.ds(at[p], part)], rows_of(ws, weights[k][p], first), NT) for p in range(parts))
                query, other = made[:, :HEAD], made[:, HEAD:]
                out[z ^ k, :, r * HEAD : (r + 1) * HEAD] = (query * cosine + swapped(query) * sine).astype(BF16)
                out[z ^ k, :, (SPANS + r) * HEAD : (SPANS + r + 1) * HEAD] = (
                    other * cos_kv + swapped(other) * sin_kv
                ).astype(BF16)

    return call(kernel, [(4, block, 8 * HEAD)], "project")(ids, *x, *arrays, *tables)[0]


def out_weights(ids, weights):
    parts = len(weights[0])
    part = weights[0][0][0].shape[-1]
    arrays, rows_of = distinct([item for items in weights for item in items])

    def kernel(ids, *refs):
        ws, (orel,) = split(refs, len(arrays), 1)
        at = offsets(ids, parts, part)
        for j in range(4):
            for p in range(parts):
                orel[j * HEAD : (j + 1) * HEAD, pl.ds(at[p], part)] = rows_of(ws, weights[j][p], slice(2 * HEAD, 3 * HEAD))

    return call(kernel, [(4 * HEAD, parts * part)], "out_weights")(ids, *arrays)[0]


def out_project(ids, pieces, orel):
    block, width = pieces.shape[1], orel.shape[1]

    def kernel(ids, pieces, orel, near, far, att):
        for j in range(4):
            for r in range(SPANS):
                att[r * block : (r + 1) * block, j * HEAD : (j + 1) * HEAD] = pieces[ids[0] ^ j, :, r * HEAD : (r + 1) * HEAD]
        for r in (1, 3, 2, 0):
            made = mm(att[r * block : (r + 1) * block, :], orel[...], NN).astype(BF16)
            (far if r % 2 else near)[r // 2] = made

    outs = [(2, block, width)] * 2 + [(4 * block, 4 * HEAD)]
    return call(kernel, outs, "out_project")(ids, pieces, orel)


def out_back(ids, grads, att, orel, parts):
    block, width = grads[0].shape
    part = width // parts

    def kernel(ids, *refs):
        gs, (att, orel), (ds,), douts, (g_s,) = split(refs, SPANS, 2, 1, parts, 1)
        at = offsets(ids, parts, part)
        for r, grad in enumerate(gs):
            g_s[r * block : (r + 1) * block, :] = grad[...]
        made = mm(g_s[...], orel[...], NT).astype(BF16)
        for r in range(SPANS):
            for j in range(4):
                ds[ids[0] ^ j, :, r * HEAD : (r + 1) * HEAD] = made[r * block : (r + 1) * block, j * HEAD : (j + 1) * HEAD]
        for p in range(parts):
            total = mm(att[...], g_s[:, pl.ds(at[p], part)], TN)
            for k in range(4):
                douts[p][k] = total[k * HEAD : (k + 1) * HEAD].astype(BF16)

    outs = [(4, block, 4 * HEAD)] + [(4, HEAD, part)] * parts
    made = call(kernel, outs, "out_back", [((4 * block, width), BF16)])(ids, *grads, att, orel)
    return made[0], made[1:]


def pack(ids, queries, mine, theirs):
    _, block, wide = queries.shape

    def kernel(ids, queries, mine, theirs, out):
        t = ids[1]
        for zj in range(4):
            out[zj, :, :wide] = queries[zj]
            for r in range(SPANS):
                rows = pl.ds(pl.multiple_of(((t ^ r) * SPANS + zj) * block, block), block)
                total = (mine[rows, :].astype(F32) + theirs[rows, :].astype(F32)).astype(BF16)
                out[zj, :, wide + r * HEAD : wide + (r + 1) * HEAD] = total[:, :HEAD]

    return call(kernel, [(4, block, 2 * wide)], "pack")(ids, queries, mine, theirs)[0]


def project_weights(ids, grads, x, parts):
    block, width = x[0].shape
    part = width // parts

    def kernel(ids, *refs):
        (grads,), xs, (d_out,), das, (x_s,) = split(refs, 1, SPANS, 1, 2 * parts, 1)
        at = offsets(ids, parts, part)
        for j in range(4):
            for r in range(SPANS):
                for half in range(2):
                    lanes = slice((half * SPANS + r) * HEAD, (half * SPANS + r + 1) * HEAD)
                    d_out[r * block : (r + 1) * block, (2 * j + half) * HEAD : (2 * j + half + 1) * HEAD] = grads[
                        ids[0] ^ j, :, lanes
                    ]
        for r, x in enumerate(xs):
            x_s[r * block : (r + 1) * block, :] = x[...]
        for p in reversed(range(parts)):
            total = mm(d_out[...], x_s[:, pl.ds(at[p], part)], TN)
            for k in range(4):
                das[2 * p + (k < 2)][k % 2] = total[2 * k * HEAD : (2 * k + 2) * HEAD].astype(BF16)

    outs = [(4 * block, 8 * HEAD)] + [(2, 2 * HEAD, part)] * (2 * parts)
    made = call(kernel, outs, "project_weights", [((4 * block, width), BF16)], 100)(ids, grads, *x)
    return made[0], made[1:]


def project_tokens(ids, grads, x, weights):
    rows = grads.shape[0]
    block = rows // SPANS
    parts = len(weights[0])
    part = weights[0][0][0].shape[-1]
    width = parts * part
    arrays, rows_of = distinct([item for items in weights for item in items])

    def kernel(ids, *refs):
        (d_s,), xs, ws, (near, far, sums), (a_s,) = split(refs, 1, SPANS, len(arrays), 3, 1)
        at = offsets(ids, parts, part)
        for j in range(4):
            for p in range(parts):
                a_s[2 * j * HEAD : (2 * j + 2) * HEAD, pl.ds(at[p], part)] = rows_of(ws, weights[j][p], slice(0, 2 * HEAD))
        total = None
        for r in (1, 3, 2, 0):
            made = mm(d_s[r * block : (r + 1) * block, :], a_s[...], NN)
            term = jnp.sum(made * xs[r][...].astype(F32), axis=0, keepdims=True)
            total = term if total is None else total + term
            (far if r % 2 else near)[r // 2] = made.astype(BF16)
        sums[...] = jnp.broadcast_to(total, (8, width))

    outs = [((2, block, width), BF16)] * 2 + [((8, width), F32)]
    return call(kernel, outs, "project_tokens", [((8 * HEAD, width), BF16)], 100)(ids, grads, *x, *arrays)


def settle_attn(ids, grads, out_sums):
    flat = [array for pair in grads for array in pair]
    each = len(grads[0])
    _, high, part = flat[0].shape
    low = out_sums.shape[1]

    def kernel(ids, *refs):
        late, early, (out_s,), outs = split(refs, each, each, 1, 4)
        for k, out in enumerate(outs):
            pair = early if k < 2 else late
            total = pair[0][k % 2]
            if each == 2:
                total = (total.astype(F32) + pair[1][k % 2].astype(F32)).astype(BF16)
            out[:high, :] = total
            out[high:, :] = out_s[k]

    return call(kernel, [(high + low, part)] * 4, "settle_attn")(ids, *flat, out_sums)


def feed(ids, x, grads, weights):
    block, width = x[0].shape
    part, units = weights[0][0].shape[-2:]
    parts = width // part
    rows, every = 2 * block, 4 * units
    arrays = list({id(item[0]): item[0] for item in weights}.values())
    index = {id(array): i for i, array in enumerate(arrays)}

    def kernel(ids, *refs):
        xs, gs, ws, ffn, two, (hid, dgate, dup), (x_s, g_s, w_s) = split(refs, 2, 2, len(arrays), 2, 2, 3, 3)
        at = [pl.multiple_of(place, LANES) for place in offsets(ids, parts, part)]
        for r in range(2):
            x_s[r * block : (r + 1) * block, :] = xs[r][...]
            g_s[r * block : (r + 1) * block, :] = gs[r][...]
        for array, where, m, k, p in weights:
            w_s[m, pl.ds(at[p], part), k * units : (k + 1) * units] = ws[index[id(array)]][where]

        def eighth(i, _):
            lanes = pl.ds(pl.multiple_of(i // 2 * units, LANES), units)
            at = pl.ds(pl.multiple_of(lax.rem(i, 2) * block, block), block)
            gate = mm(x_s[at, :], w_s[0, :, lanes], NN)
            up = mm(x_s[at, :], w_s[1, :, lanes], NN)
            back = mm(g_s[at, :], w_s[2, :, lanes], NN)
            sigma = 0.5 * jnp.tanh(0.5 * gate) + 0.5
            swish = gate * sigma
            hid[at, lanes] = (swish * up).astype(BF16)
            dup[at, lanes] = (back * swish).astype(BF16)
            dgate[at, lanes] = (back * up * (sigma + swish * (1.0 - sigma))).astype(BF16)
            return 0

        lax.fori_loop(0, 8, eighth, 0)
        cut = width // 3

        def third(p, _):
            lanes = pl.ds(pl.multiple_of(p * cut, LANES), cut)
            made = mm(dgate[...], w_s[0, lanes, :], NT) + mm(dup[...], w_s[1, lanes, :], NT)
            for r in range(2):
                two[r][:, lanes] = made[r * block : (r + 1) * block].astype(BF16)
            made = mm(hid[...], w_s[2, lanes, :], NT)
            for r in range(2):
                ffn[r][:, lanes] = made[r * block : (r + 1) * block].astype(BF16)
            return 0

        lax.fori_loop(0, 3, third, 0)

    outs = [(block, width)] * 4 + [(rows, every)] * 3
    scratch = [((rows, width), BF16), ((rows, width), BF16), ((3, width, every), BF16)]
    made = call(kernel, outs, "feed", scratch, 18, 34)(ids, *x, *grads, *arrays)
    return made[:2], made[2:4], made[4:]


def feed_weights(ids, x, grads, near, far, parts):
    block, width = x[0].shape
    part = width // parts
    half, every = near[0].shape
    units = every // 4

    def kernel(ids, *refs):
        xs, gs, ns, fs, outs, (rows_s, h_s) = split(refs, SPANS, SPANS, 3, 3, 4 * parts, 2)
        at = offsets(ids, parts, part)
        for r in range(SPANS):
            rows_s[0, r * block : (r + 1) * block, :] = xs[r][...]
            rows_s[1, r * block : (r + 1) * block, :] = gs[r][...]
        for m in range(3):
            h_s[m, :half] = ns[m][...]
            h_s[m, half:] = fs[m][...]

        def one(m, _):
            side = lax.rem(m + 1, 3)
            left = m // 2
            for p in reversed(range(parts)):
                total = mm(rows_s[left, :, pl.ds(at[p], part)], h_s[side], TN)
                for k in range(4):
                    outs[k * parts + p][m] = total[:, k * units : (k + 1) * units].astype(BF16)
            return 0

        lax.fori_loop(0, 3, one, 0)

    outs = [(3, part, units)] * (4 * parts)
    scratch = [((2, 4 * block, width), BF16), ((3, 4 * block, every), BF16)]
    return call(kernel, outs, "feed_weights", scratch, 17, 40)(ids, *x, *grads, *near, *far)


def finish_ffn(ids, pieces, gain):
    _, shard, units = pieces[0].shape
    every = SPANS * units

    def kernel(ids, *refs):
        pieces, (gain,), (gate, up, down) = split(refs, SPANS, 1, 3)
        scale = gain[...]
        for r, piece in enumerate(pieces):
            lanes = pl.ds(pl.multiple_of((ids[1] ^ r) * units, LANES), units)
            gate[:, lanes] = piece[0].astype(F32) * scale
            up[:, lanes] = piece[1].astype(F32) * scale
            down[:, lanes] = piece[2].astype(F32)

    return call(kernel, [((shard, every), F32)] * 3, "finish_ffn")(ids, *pieces, gain)


def finish_attn(ids, pieces, gain):
    shard = pieces[0].shape[1]

    def kernel(ids, *refs):
        pieces, (gain,), (query, key, value, out_w), (made,) = split(refs, SPANS, 1, 4, 1)
        scale = gain[...]
        for r, piece in enumerate(pieces):
            made[ids[1] ^ r] = piece[...].astype(F32)
        for place in range(SPANS):
            lanes = slice(place * HEAD, (place + 1) * HEAD)
            half = slice(place // 2 * HEAD, (place // 2 + 1) * HEAD)
            out_w[:, lanes] = jnp.transpose(made[place, 2 * HEAD :])
            query[:, lanes] = jnp.transpose(made[place, :HEAD]) * scale
            (value if place % 2 else key)[:, half] = jnp.transpose(made[place, HEAD : 2 * HEAD]) * scale

    outs = [((shard, wide * HEAD), F32) for wide in (4, 2, 2, 4)]
    scratch = [((SPANS, 3 * HEAD, shard), F32)]
    return call(kernel, outs, "finish_attn", scratch)(ids, *pieces, gain)


def swap(value, axis):
    return lax.ppermute(value, axis, [(0, 1), (1, 0)])


def sent(value, axis, bits):
    return lax.ppermute(value, axis, [(i, i ^ bits) for i in range(lax.axis_size(axis))])


def gather_group(value):
    core = swap(value, "c")
    across = swap(value, "x")
    return value, core, across, swap(across, "c")


def scatter_group(near, far):
    total = near.astype(F32) + swap(far, "c").astype(F32)
    return total[0] + swap(total[1].astype(BF16), "x").astype(F32)


def scatter_halves(near, far):
    far_total = far[0].astype(F32) + swap(far[1], "c").astype(F32)
    crossing = swap(far_total.astype(BF16), "x")
    return near[0].astype(F32) + swap(near[1], "c").astype(F32) + crossing.astype(F32)


def exchange(pieces):
    return lax.all_to_all(pieces, "z", split_axis=0, concat_axis=0, tiled=True)


def spread(pieces):
    return [
        pieces[0],
        swap(pieces[1], "c"),
        swap(pieces[2], "x"),
        lax.ppermute(pieces[3], ("x", "c"), [(i, 3 - i) for i in range(SPANS)]),
    ]


def beside(mine, dim):
    if lax.axis_size("y") == 2:
        return [mine, swap(mine, "y")]
    return [lax.all_gather(mine, "y", axis=dim, tiled=True)]


def along_z(mine):
    if lax.axis_size("z") != 4:
        return [mine] + [sent(mine, "z", k) for k in range(1, lax.axis_size("z"))]
    far = sent(mine, "z", 3)
    return [mine, sent(mine, "z", 1), sent(far, "z", 1), far]


def onto_z(pieces):
    far = pieces[3].astype(F32) + sent(pieces[2], "z", 1).astype(F32)
    near = pieces[0].astype(F32) + sent(pieces[1], "z", 1).astype(F32)
    return (near + sent(far.astype(BF16), "z", 3).astype(F32)).astype(BF16)


def settled(pieces, parts, dim):
    if parts == 2:
        sums = [
            (pieces[2 * k].astype(F32) + swap(pieces[2 * k + 1], "y").astype(F32)).astype(BF16) for k in range(4)
        ]
    else:
        sums = [lax.psum_scatter(piece, "y", scatter_dimension=dim, tiled=True) for piece in pieces]
    return onto_z(sums)


def halved(values, rest, axis, dim):
    if lax.axis_size(axis) != 2:
        values, rest = lax.psum((values, rest), axis)
        return lax.dynamic_index_in_dim(values, lax.axis_index(axis), dim, keepdims=False), rest
    here = lax.axis_index(axis)
    kept = lax.dynamic_index_in_dim(values, here, dim, keepdims=False)
    gone = lax.dynamic_index_in_dim(values, 1 - here, dim, keepdims=False)
    came = swap(jnp.concatenate([gone.reshape(-1), rest]), axis)
    return kept + came[: kept.size].reshape(kept.shape), rest + came[kept.size :]


def over_z(value):
    return value + sum(sent(value, "z", k) for k in range(1, lax.axis_size("z")))


def unit(values):
    scale = lax.rsqrt(jnp.mean(values * values, axis=-1, keepdims=True) + EPSILON)
    return values * scale, scale


def unit_back(values, scale, grad):
    inner = jnp.mean(grad * values, axis=-1, keepdims=True)
    return scale * grad - values * (scale * scale * scale) * inner


def per_device(tokens, w_query, w_key, w_value, w_out, w_gate, w_up, w_down, norm_attn, norm_ffn, grad_out):
    sequences, count = lax.axis_size("y"), lax.axis_size("z")
    parts = 2 if sequences == 2 else 1
    block, width = tokens.shape
    shard = w_query.shape[0]
    t = lax.axis_index("x") * 2 + lax.axis_index("c")
    ids = jnp.stack([lax.axis_index("z"), t, lax.axis_index("y")]).astype(jnp.int32)
    gain_attn = norm_attn.astype(F32)[:, None]
    gain_ffn = norm_ffn.astype(F32)[:, None]

    fence = lax.optimization_barrier

    resid = tokens.astype(F32)
    unit_one, scale_one = unit(resid)
    attn_pieces, low_one = fence((prepare_attn(ids, w_query, w_key, w_value, w_out, gain_attn), unit_one.astype(BF16)))
    attn_mine = join_attn(ids, spread(attn_pieces))
    lane = jnp.arange(LANES)
    freq = ROPE_BASE ** (-(lane % (HEAD // 2) * 2.0) / HEAD)
    inner = jnp.arange(block, dtype=F32)[:, None] * freq
    outer = (jnp.arange(SEQUENCE_LENGTH // block, dtype=F32) * block)[:, None] * freq
    sign = jnp.where(lane < HEAD // 2, -1.0, 1.0)
    tables = (jnp.cos(inner), jnp.sin(inner) * sign, jnp.cos(outer), jnp.sin(outer) * sign)
    attn_mine, ffn_pieces, tables, low_one = fence(
        (attn_mine, prepare_ffn(ids, w_gate, w_up, w_down, gain_ffn), tables, low_one)
    )

    attn_three, attn_one = sent(attn_mine, "z", 3), sent(attn_mine, "z", 1)
    own = beside(attn_mine, 1)
    ffn_mine = join_ffn(ids, spread(ffn_pieces))
    core, across = swap(low_one, "c"), swap(low_one, "x")
    ffn_mine, attn_three, attn_one, own = fence((ffn_mine, attn_three, attn_one, own))
    attn_two = sent(attn_three, "z", 1)
    three_one = beside(jnp.stack([attn_three, attn_one]), 2)
    gate_three = sent(ffn_mine[0], "z", 3)
    attn_two, three_one, gate_three, ffn_mine, core, across = fence(
        (attn_two, three_one, gate_three, ffn_mine, core, across)
    )
    x_one = (low_one, core, across, swap(across, "c"))
    two = beside(attn_two, 1)
    attn_weights = [
        [(array, ()) for array in own],
        [(array, (1,)) for array in three_one],
        [(array, ()) for array in two],
        [(array, (0,)) for array in three_one],
    ]
    gate_one, up_three = sent(ffn_mine[0], "z", 1), sent(ffn_mine[1], "z", 3)
    made = project(ids, x_one, attn_weights, tables)
    made, gate_one, up_three, gate_three, ffn_mine, grad_in = fence(
        (made, gate_one, up_three, gate_three, ffn_mine, grad_out)
    )

    made = exchange(made)
    ffn_own = beside(ffn_mine, 1)
    g_rows = gather_group(grad_in)
    by_one = jnp.stack([ffn_mine[1], gate_three])
    first = jnp.stack([gate_three, gate_one, up_three])
    made, ffn_own, g_rows, by_one, first, down_mine, orel = fence(
        (made, ffn_own, g_rows, by_one, first, ffn_mine[2], out_weights(ids, attn_weights))
    )
    by_one, down_three = sent(by_one, "z", 1), sent(down_mine, "z", 3)
    first = beside(first, 1)
    other = swap(made[:, :, SPANS * HEAD :], "c")
    attended, q_seq, kv_seq, o_seq, lse = attend(ids, made, other)
    attended, down_three, by_one, first, up_three, down_mine = fence(
        (attended, down_three, by_one, first, up_three, down_mine)
    )
    attended = exchange(attended)
    by_one = beside(by_one, 1)
    down_one = sent(down_mine, "z", 1)
    both_two = jnp.stack([up_three, down_three])
    attended, by_one, down_one, down_three, both_two = fence((attended, by_one, down_one, down_three, both_two))
    both_two = sent(both_two, "z", 1)
    down_three, down_one = beside(down_three, 0), beside(down_one, 0)
    near, far, att = out_project(ids, attended, orel)
    branch_attn = scatter_group(near, far)
    state = resid + branch_attn
    unit_two, scale_two = unit(state)
    low_two, both_two, down_three, down_one = fence((unit_two.astype(BF16), both_two, down_three, down_one))
    x_two = gather_group(low_two)
    both_two = beside(both_two, 1)
    x_two, both_two = fence((x_two, both_two))

    ffn_weights = []
    for p in range(parts):
        ffn_weights += [(ffn_own[p], (m,), m, 0, p) for m in range(3)]
        ffn_weights += [(first[p], (i,), *place, p) for i, place in enumerate(((0, 3), (0, 1), (1, 3)))]
        ffn_weights += [(by_one[p], (i,), *place, p) for i, place in enumerate(((1, 1), (0, 2)))]
        ffn_weights += [(down_three[p], (Ellipsis,), 2, 3, p), (down_one[p], (Ellipsis,), 2, 1, p)]
        ffn_weights += [(both_two[p], (0,), 1, 2, p), (both_two[p], (1,), 2, 2, p)]
    ffn_far, two_far, kept_far = feed(ids, x_two[2:], g_rows[2:], ffn_weights)
    crossing = (two_far[0].astype(F32) + swap(two_far[1], "c").astype(F32)).astype(BF16)
    crossing, x_near = fence((crossing, x_two[:2]))
    crossing = swap(crossing, "x")
    ffn_near, two_near, kept_near = feed(ids, x_near, g_rows[:2], ffn_weights)
    two_near, crossing = fence((two_near, crossing))
    grad_unit_two = two_near[0].astype(F32) + swap(two_near[1], "c").astype(F32) + crossing.astype(F32)
    grad_state = grad_out.astype(F32) + unit_back(state, scale_two, grad_unit_two)
    state_low, kept_near, ffn_near, ffn_far, grad_unit_two = fence(
        (grad_state.astype(BF16), kept_near, ffn_near, ffn_far, grad_unit_two)
    )
    across, core = swap(state_low, "x"), swap(state_low, "c")
    feed_grads = feed_weights(ids, x_two, g_rows, kept_near, kept_far, parts)
    across, core, feed_grads = fence((across, core, feed_grads))
    g_state = (state_low, core, across, swap(across, "c"))

    def home(total):
        pieces = total.reshape(*total.shape[:-2], SPANS, shard, total.shape[-1])
        return spread([lax.dynamic_index_in_dim(pieces, t ^ r, pieces.ndim - 3, keepdims=False) for r in range(SPANS)])

    def crossed(grads, k):
        if parts == 1:
            return lax.psum_scatter(grads[k], "y", scatter_dimension=1, tiled=True)
        return swap(grads[2 * k + 1], "y")

    def added(grads, k, came):
        return came if parts == 1 else (grads[2 * k].astype(F32) + came.astype(F32)).astype(BF16)

    two_came = crossed(feed_grads, 2)
    grad_att, out_grads = out_back(ids, g_state, att, orel, parts)
    grad_att = exchange(grad_att)
    onward = added(feed_grads, 2, two_came)
    grad_att, onward, feed_grads, out_grads = fence((grad_att, onward, feed_grads, out_grads))
    onward = sent(onward, "z", 1)
    three_came = crossed(feed_grads, 3)
    if parts == 2:
        out_sums = out_grads[0].astype(F32) + swap(out_grads[1], "y").astype(F32)
    else:
        out_sums = lax.psum_scatter(out_grads[0], "y", scatter_dimension=2, tiled=True)
    dq, keep, give = attend_back(ids, q_seq, kv_seq, o_seq, lse, tables, grad_att)
    dq, keep, give, onward, three_came, feed_grads, ffn_near, ffn_far, out_sums = fence(
        (dq, keep, give, onward, three_came, feed_grads, ffn_near, ffn_far, out_sums.astype(BF16))
    )
    one_came = crossed(feed_grads, 1)
    grads_heads = exchange(pack(ids, dq, keep, swap(give, "c")))
    branch_ffn = scatter_halves(ffn_near, ffn_far)
    result = state + branch_ffn
    gain_two = jnp.sum(grad_unit_two * unit_two, axis=0)
    squares = jnp.stack([jnp.sum(result * result), jnp.sum(branch_attn * branch_attn), jnp.sum(branch_ffn * branch_ffn)])
    onward = (added(feed_grads, 3, three_came).astype(F32) + onward.astype(F32)).astype(BF16)
    onward, onward_down = onward[:2], onward[2:]
    one_sum = added(feed_grads, 1, one_came)
    grads_heads, result, squares, gain_two, onward, onward_down, one_sum, feed_grads = fence(
        (grads_heads, result, squares, gain_two, onward, onward_down, one_sum, feed_grads)
    )
    onward = sent(onward, "z", 3)
    feed_one = sent(one_sum, "z", 1)
    grads_qkv, qkv_grads = project_weights(ids, grads_heads, x_one, parts)
    grads_qkv, qkv_grads = fence((grads_qkv, qkv_grads))
    near, far, gain_one = project_tokens(ids, grads_qkv, x_one, attn_weights)
    if parts == 2:
        gone = [(kept, swap(piece, "y")) for kept, piece in zip(qkv_grads[:2], qkv_grads[2:])]
    else:
        gone = [(lax.psum_scatter(piece, "y", scatter_dimension=2, tiled=True),) for piece in qkv_grads]
    own_came = crossed(feed_grads, 0)
    gains = jnp.stack([gain_one[0], gain_two]).reshape(2, sequences, 2, 2, shard)
    sums = settle_attn(ids, gone, out_sums)
    sums, feed_grads, onward, onward_down, feed_one, near, far, own_came, gains = fence(
        (sums, feed_grads, onward, onward_down, feed_one, near, far, own_came, gains)
    )
    onto_three = (sums[3].astype(F32) + sent(sums[2], "z", 1).astype(F32)).astype(BF16)
    onto_one = sent(sums[1], "z", 1)
    onward_down = sent(onward_down, "z", 3)
    total = near.astype(F32) + swap(far, "c").astype(F32)
    gains, squares = halved(gains, squares, "c", 3)
    crossing = swap(total[1].astype(BF16), "x")
    gains, squares = halved(gains, squares, "y", 1)
    feed_total = added(feed_grads, 0, own_came).astype(F32) + jnp.concatenate([onward, onward_down]).astype(F32)
    feed_total = (feed_total + feed_one.astype(F32)).astype(BF16)
    onto_three, onto_one, crossing, feed_total, gains, squares = fence(
        (onto_three, onto_one, crossing, feed_total, gains, squares)
    )
    onto_three = sent(onto_three, "z", 3)
    feed_home = home(feed_total)
    grad_unit_one = total[0] + crossing.astype(F32)
    grad_tokens = (grad_state + unit_back(resid, scale_one, grad_unit_one)).astype(BF16)
    gains, squares = halved(gains, squares, "x", 1)
    onto_three, onto_one, feed_home, gains, squares, grad_tokens = fence(
        (onto_three, onto_one, feed_home, gains, squares, grad_tokens)
    )
    attn_home = spread(part_attn(ids, sums[0], onto_one, onto_three))
    attn_home, gains, squares = fence((attn_home, gains, squares))
    totals = over_z(jnp.concatenate([gains.reshape(-1), squares]))
    grad_gate, grad_up, grad_down = finish_ffn(ids, feed_home, gain_ffn)
    grad_query, grad_key, grad_value, grad_outproj = finish_attn(ids, attn_home, gain_attn)
    entries = block * width * sequences * SPANS * count
    return (
        result.astype(BF16),
        grad_tokens,
        grad_query,
        grad_key,
        grad_value,
        grad_outproj.T,
        grad_gate,
        grad_up,
        grad_down.T,
        totals[:shard] / gain_attn[:, 0],
        totals[shard : 2 * shard] / gain_ffn[:, 0],
        jnp.sqrt(totals[2 * shard :] / entries),
    )


def solution(mesh):
    fsdp, tensor = mesh.shape["fsdp"], mesh.shape["tensor"]
    split = Mesh(mesh.devices.reshape(fsdp // SPANS, 2, 2, tensor), ("y", "x", "c", "z"))
    rows = ("y", "x", "c")
    tok = P(("y", "x", "c", "z"), None)
    col, row, vec = P(rows, "z"), P("z", rows), P(rows)
    return jax.shard_map(
        per_device,
        mesh=split,
        in_specs=(tok, col, col, col, row, col, col, row, vec, vec, tok),
        out_specs=(tok, tok, col, col, col, row, col, col, row, vec, vec, P()),
        check_vma=False,
    )
```

profile of v0, /device:TPU:0, one launch (start us, length us, event | category | flops | bytes accessed | tf_op | source)
XLA Modules:
  0.0 575.5 jit_solution(4827415533851406183)
XLA Ops:
  25.4 8.4 %collective-permute-done.4.refs_2_ = bf16[3,192,256]{2,1,0:T(8,128)(2,1)S(1)} collective-permute-done((bf16[3,192,256]{2,1,0:T(8,128)(2,1)S(1)}, bf16[3,192,256]{2,1,0:T(8,128)(2,1)S(1)}, u32[]{:S(2)}, u32[]{:S(2)}) %collective-permute-start.4) | collective-permute-done | bytes 294944 | tf_op jit(solution)/shard_map/ppermute | solution.py:627
  47.9 16.3 %collective-permute-done.13.refs_2_.refs_3_ = bf16[256,1536]{1,0:T(8,128)(2,1)S(1)} collective-permute-done((bf16[256,1536]{1,0:T(8,128)(2,1)S(1)}, bf16[256,1536]{1,0:T(8,128)(2,1)S(1)}, u32[]{:S(2)}, u32[]{:S(2)}) %collective-permute-start.13) | collective-permute-done | bytes 786464 | tf_op jit(solution)/shard_map/ppermute | solution.py:627
  71.4 8.6 %collective-permute-done.15.refs_9_.refs_5_.refs_10_ = bf16[288,768]{1,0:T(8,128)(2,1)S(1)} collective-permute-done((bf16[288,768]{1,0:T(8,128)(2,1)S(1)}, bf16[288,768]{1,0:T(8,128)(2,1)S(1)}, u32[]{:S(2)}, u32[]{:S(2)}) %collective-permute-start.15) | collective-permute-done | bytes 442400 | tf_op jit(solution)/shard_map/ppermute | solution.py:627
  80.0 5.1 project.1
  89.5 4.8 all-to-all-start
  96.4 17.3 %collective-permute-done.20.refs_2_.refs_6_ = bf16[256,1536]{1,0:T(8,128)(2,1)S(1)} collective-permute-done((bf16[256,1536]{1,0:T(8,128)(2,1)}, bf16[256,1536]{1,0:T(8,128)(2,1)S(1)}, u32[]{:S(2)}, u32[]{:S(2)}) %collective-permute-start.20) | collective-permute-done | bytes 786464 | tf_op jit(solution)/shard_map/ppermute | solution.py:627
  126.8 4.6 all-to-all-done.own
  135.9 18.7 %attend.1 = (bf16[4,256,384]{2,1,0:T(8,128)(2,1)S(1)}, bf16[4096,128]{1,0:T(8,128)(2,1)S(1)}, bf16[2,4096,128]{2,1,0:T(8,128)(2,1)S(1)}, bf16[4096,128]{1,0:T(8,128)(2,1)S(1)}, f32[8,4096]{1,0:T(8,128)S(1)}) custom-call(s32[3]{0:T(128)S(1)} %pad_add_fusion.ids, bf16[4,256,768]{2,1,0:T(8,128)(2,1)} %all-to-all-done.own, ...), custom_call_target="tpu_custom_call" | custom-call | flops 20999999488 | bytes 1 | tf_op jit(solution)/shard_map/attend/pallas_call | solution.py:112
  164.6 4.4 all-to-all-start.1
  173.6 18.7 %collective-permute-done.27.refs_8_ = bf16[768,256]{1,0:T(8,128)(2,1)} collective-permute-done((bf16[768,256]{1,0:T(8,128)(2,1)}, bf16[768,256]{1,0:T(8,128)(2,1)}, u32[]{:S(2)}, u32[]{:S(2)}) %collective-permute-start.27) | collective-permute-done | bytes 393248 | tf_op jit(solution)/shard_map/ppermute | solution.py:631
  203.8 16.3 %collective-permute-done.29 = bf16[256,1536]{1,0:T(8,128)(2,1)S(1)} collective-permute-done((bf16[256,1536]{1,0:T(8,128)(2,1)S(1)}, bf16[256,1536]{1,0:T(8,128)(2,1)S(1)}, u32[]{:S(2)}, u32[]{:S(2)}) %collective-permute-start.29) | collective-permute-done | bytes 786464 | tf_op jit(solution)/shard_map/ppermute | solution.py:627
  222.7 17.7 %collective-permute-done.34.refs_0_.refs_2_ = bf16[256,1536]{1,0:T(8,128)(2,1)S(1)} collective-permute-done((bf16[256,1536]{1,0:T(8,128)(2,1)S(1)}, bf16[256,1536]{1,0:T(8,128)(2,1)S(1)}, u32[]{:S(2)}, u32[]{:S(2)}) %collective-permute-start.34) | collective-permute-done | bytes 786464 | tf_op jit(solution)/shard_map/ppermute | solution.py:627
  242.8 15.6 %feed.2 = (bf16[256,1536]{1,0:T(8,128)(2,1)S(1)}, bf16[256,1536]{1,0:T(8,128)(2,1)}, bf16[256,1536]{1,0:T(8,128)(2,1)S(1)}, bf16[256,1536]{1,0:T(8,128)(2,1)S(1)...) custom-call(s32[3]{0:T(128)S(1)} %pad_add_fusion.ids, ...), custom_call_target="tpu_custom_call" | custom-call | flops 18000001024 | bytes 1 | tf_op jit(solution)/shard_map/feed/pallas_call | solution.py:229
  263.6 15.2 %feed.3 = (bf16[256,1536]{1,0:T(8,128)(2,1)S(1)}, bf16[256,1536]{1,0:T(8,128)(2,1)S(1)}, bf16[256,1536]{1,0:T(8,128)(2,1)S(1)}, bf16[256,1536]{1,0:T(8,128)(2,1)...) custom-call(s32[3]{0:T(128)S(1)} %pad_add_fusion.ids, ...), custom_call_target="tpu_custom_call" | custom-call | flops 18000001024 | bytes 1 | tf_op jit(solution)/shard_map/feed/pallas_call | solution.py:229
  290.7 14.5 %feed_weights.1 = (bf16[3,768,256]{2,1,0:T(8,128)(2,1)S(1)}, bf16[3,768,256]{2,1,0:T(8,128)(2,1)}, bf16[3,768,256]{2,1,0:T(8,128)(2,1)}, bf16[3,768,256]{2,1,0:T...) custom-call(s32[3]{0:T(128)S(1)} %pad_add_fusion.ids, ...), custom_call_target="tpu_custom_call" | custom-call | flops 17000000512 | bytes 1 | tf_op jit(solution)/shard_map/feed_weights/pallas_call | solution.py:229
  305.3 4.1 collective-permute-done.40.refs_2_
  318.0 4.6 all-to-all-start.2
  322.6 15.5 %collective-permute-done.43 = bf16[3,768,256]{2,1,0:T(8,128)(2,1)} collective-permute-done((bf16[3,768,256]{2,1,0:T(8,128)(2,1)}, bf16[3,768,256]{2,1,0:T(8,128)(2,1)}, u32[]{:S(2)}, u32[]{:S(2)}) %collective-permute-start.43) | collective-permute-done | bytes 1179680 | tf_op jit(solution)/shard_map/ppermute | solution.py:627
  349.0 35.0 %attend_back.1 = (bf16[4,256,384]{2,1,0:T(8,128)(2,1)S(1)}, bf16[4096,128]{1,0:T(8,128)(2,1)S(1)}, bf16[4096,128]{1,0:T(8,128)(2,1)S(1)}) custom-call(s32[3]{0:T(128)S(1)} %pad_add_fusion.ids, bf16[4096,128]{1,0:T(8,128)(2,1)S(1)} %copy-done.87, bf16[2,4096,128]{2,1,0:T(8,128)(2,1)S(1)} %copy-done.85, bf16[4096,128]{1,0:T(8,128)(2,1)S(1)} %copy-done.89, ...), custom_call_target="tpu_custom_call" | custom-call | flops 38999998464 | bytes 1 | tf_op jit(solution)/shard_map/attend_back/pallas_call | solution.py:201
  389.9 4.6 all-to-all-start.3
  401.5 21.4 %collective-permute-done.51 = bf16[3,768,256]{2,1,0:T(8,128)(2,1)S(1)} collective-permute-done((bf16[3,768,256]{2,1,0:T(8,128)(2,1)}, bf16[3,768,256]{2,1,0:T(8,128)(2,1)S(1)}, u32[]{:S(2)}, u32[]{:S(2)}) %collective-permute-start.51) | collective-permute-done | bytes 1179680 | tf_op jit(solution)/shard_map/ppermute | solution.py:627
  435.4 5.8 %project_weights.1 = (bf16[1024,768]{1,0:T(8,128)(2,1)S(1)}, bf16[2,192,768]{2,1,0:T(8,128)(2,1)S(1)}, bf16[2,192,768]{2,1,0:T(8,128)(2,1)S(1)}, bf16[2,192,768]{2,1,0:T(8,128)(2,1)}, bf16[2,192,768]{2,1,0:T(8,128)(2,1)}) custom-call(s32[3]{0:T(128)S(1)} %pad_add_fusion.ids, bf16[4,256,768]{2,1,0:T(8,128)(2,1)} %all-to-all-done.3.refs_0_, ...), custom_call_target="tpu_custom_call" | custom-call | flops 99999997952 | bytes 1 | tf_op jit(solution)/shard_map/project_weights/pallas_call | solution.py:229
  451.5 6.3 %collective-permute-done.52.refs_1_ = bf16[2,192,768]{2,1,0:T(8,128)(2,1)} collective-permute-done((bf16[2,192,768]{2,1,0:T(8,128)(2,1)}, bf16[2,192,768]{2,1,0:T(8,128)(2,1)}, u32[]{:S(2)}, u32[]{:S(2)}) %collective-permute-start.52) | collective-permute-done | bytes 589856 | tf_op jit(solution)/shard_map/ppermute | solution.py:627
  457.9 12.6 %collective-permute-done.53.refs_3_ = bf16[2,192,768]{2,1,0:T(8,128)(2,1)} collective-permute-done((bf16[2,192,768]{2,1,0:T(8,128)(2,1)}, bf16[2,192,768]{2,1,0:T(8,128)(2,1)}, u32[]{:S(2)}, u32[]{:S(2)}) %collective-permute-start.53) | collective-permute-done | bytes 589856 | tf_op jit(solution)/shard_map/ppermute | solution.py:627
  477.3 10.1 %collective-permute-done.54 = bf16[2,768,256]{2,1,0:T(8,128)(2,1)} collective-permute-done((bf16[2,768,256]{2,1,0:T(8,128)(2,1)}, bf16[2,768,256]{2,1,0:T(8,128)(2,1)}, u32[]{:S(2)}, u32[]{:S(2)}) %collective-permute-start.54) | collective-permute-done | bytes 786464 | tf_op jit(solution)/shard_map/ppermute | solution.py:631
  487.4 6.6 %collective-permute-done.56 = bf16[3,768,256]{2,1,0:T(8,128)(2,1)} collective-permute-done((bf16[3,768,256]{2,1,0:T(8,128)(2,1)}, bf16[3,768,256]{2,1,0:T(8,128)(2,1)}, u32[]{:S(2)}, u32[]{:S(2)}) %collective-permute-start.56) | collective-permute-done | bytes 1179680 | tf_op jit(solution)/shard_map/ppermute | solution.py:627
  505.5 6.7 %collective-permute-done.61 = bf16[1,768,256]{2,1,0:T(8,128)(2,1)} collective-permute-done((bf16[1,768,256]{2,1,0:T(8,128)(2,1)}, bf16[1,768,256]{2,1,0:T(8,128)(2,1)}, u32[]{:S(2)}, u32[]{:S(2)}) %collective-permute-start.61) | collective-permute-done | bytes 393248 | tf_op jit(solution)/shard_map/ppermute | solution.py:631
  514.8 6.0 %collective-permute-done.57 = bf16[288,768]{1,0:T(8,128)(2,1)} collective-permute-done((bf16[288,768]{1,0:T(8,128)(2,1)}, bf16[288,768]{1,0:T(8,128)(2,1)}, u32[]{:S(2)}, u32[]{:S(2)}) %collective-permute-start.57) | collective-permute-done | bytes 442400 | tf_op jit(solution)/shard_map/ppermute | solution.py:631
  521.9 8.1 %collective-permute-done.58.one = bf16[288,768]{1,0:T(8,128)(2,1)S(1)} collective-permute-done((bf16[288,768]{1,0:T(8,128)(2,1)}, bf16[288,768]{1,0:T(8,128)(2,1)S(1)}, u32[]{:S(2)}, u32[]{:S(2)}) %collective-permute-start.58) | collective-permute-done | bytes 442400 | tf_op jit(solution)/shard_map/ppermute | solution.py:631
  543.2 5.5 collective-permute-done.67.refs_3_
  552.1 4.8 collective-permute-done.70.refs_2_
  559.3 7.9 %collective-permute-start.72 = (f32[387]{0:T(512)S(1)}, f32[387]{0:T(512)S(1)}, u32[]{:S(2)}, u32[]{:S(2)}) collective-permute-start(f32[387]{0:T(512)S(1)} %constant_dynamic-update-slice_fusion), channel_id=1, source_target_pairs={{0,1},{1,0},{2,3},{3,2},{4,5},{5,4},{6,7},{7,6},{8,9},{9,8},{10,11... | collective-permute-start | bytes 4652 | tf_op jit(solution)/shard_map/ppermute | solution.py:631
  (461 shorter events, 221.5 us)
Async XLA Ops:
  22.4 20.2 %collective-permute-start.7 = (bf16[288,768]{1,0:T(8,128)(2,1)S(1)}, bf16[288,768]{1,0:T(8,128)(2,1)S(1)}, u32[]{:S(2)}, u32[]{:S(2)}) collective-permute-start(bf16[288,768]{1,0:T(8,128)(2,1)S(1)} %join_attn.1.refs_4_.refs_0_.refs_5_), channel_id=1, source_target_pairs={{0,1},{1,0},{2,3},{3,2},{4,5},{5,4},{6,7},{7,6},{8,9},{9,8},{10,11... | collective-permute-start | bytes 1327112 | tf_op jit(solution)/shard_map/ppermute | solution.py:631
  22.4 20.2 %collective-permute-start.8 = (bf16[288,768]{1,0:T(8,128)(2,1)S(1)}, bf16[288,768]{1,0:T(8,128)(2,1)S(1)}, u32[]{:S(2)}, u32[]{:S(2)}) collective-permute-start(bf16[288,768]{1,0:T(8,128)(2,1)S(1)} %join_attn.1.refs_4_.refs_0_.refs_5_), channel_id=1, source_target_pairs={{0,16},{16,0},{1,17},{17,1},{2,18},{18,2},{3,19},{19,3},{4,20},{20... | collective-permute-start | bytes 1327112 | tf_op jit(solution)/shard_map/ppermute | solution.py:627
  42.7 24.0 %collective-permute-start.10 = (bf16[2,288,768]{2,1,0:T(8,128)(2,1)S(1)}, bf16[2,288,768]{2,1,0:T(8,128)(2,1)S(1)}, u32[]{:S(2)}, u32[]{:S(2)}) collective-permute-start(bf16[2,288,768]{2,1,0:T(8,128)(2,1)S(1)} %pad_maximum_fusion.1.refs_6_.refs_2_.refs_7_), channel_id=1, source_target_pairs={{0,16},{16,0},{1,17},{17,1},{2,18},{18,2},{3,19},{19,3},{4,20},{20... | collective-permute-start | bytes 2654216 | tf_op jit(solution)/shard_map/ppermute | solution.py:627
  44.2 20.0 %collective-permute-start.13 = (bf16[256,1536]{1,0:T(8,128)(2,1)S(1)}, bf16[256,1536]{1,0:T(8,128)(2,1)S(1)}, u32[]{:S(2)}, u32[]{:S(2)}) collective-permute-start(bf16[256,1536]{1,0:T(8,128)(2,1)S(1)} %fusion.1.refs_0_.refs_1_), channel_id=1, source_target_pairs={{0,8},{8,0},{1,9},{9,1},{2,10},{10,2},{3,11},{11,3},{4,12},{12,4},... | collective-permute-start | bytes 2359304 | tf_op jit(solution)/shard_map/ppermute | solution.py:627
  45.7 20.9 %collective-permute-start.9 = (bf16[288,768]{1,0:T(8,128)(2,1)S(1)}, bf16[288,768]{1,0:T(8,128)(2,1)S(1)}, u32[]{:S(2)}, u32[]{:S(2)}) collective-permute-start(bf16[288,768]{1,0:T(8,128)(2,1)S(1)} %collective-permute-done.6), channel_id=1, source_target_pairs={{0,1},{1,0},{2,3},{3,2},{4,5},{5,4},{6,7},{7,6},{8,9},{9,8},{10,11... | collective-permute-start | bytes 1327112 | tf_op jit(solution)/shard_map/ppermute | solution.py:631
  68.6 20.8 %collective-permute-start.17 = (bf16[768,256]{1,0:T(8,128)(2,1)S(1)}, bf16[768,256]{1,0:T(8,128)(2,1)}, u32[]{:S(2)}, u32[]{:S(2)}) collective-permute-start(bf16[768,256]{1,0:T(8,128)(2,1)S(1)} %get-tuple-element.485), channel_id=1, source_target_pairs={{0,3},{1,2},{2,1},{3,0},{4,7},{5,6},{6,5},{7,4},{8,11},{9,10},{10,... | collective-permute-start | bytes 1179656 | tf_op jit(solution)/shard_map/ppermute | solution.py:631
  89.5 41.9 %all-to-all-start = ((bf16[4,256,768]{2,1,0:T(8,128)(2,1)}), bf16[4,256,768]{2,1,0:T(8,128)(2,1)}, u32[]{:S(2)}, u32[]{:S(2)}) async-start(bf16[4,256,768]{2,1,0:T(8,128)(2,1)} %copy-done), calls=%async_computation | async-start | bytes 3145728 | tf_op jit(solution)/shard_map/all_to_all | solution.py:652
  94.9 30.0 %collective-permute-start.18 = (bf16[3,768,256]{2,1,0:T(8,128)(2,1)S(1)}, bf16[3,768,256]{2,1,0:T(8,128)(2,1)S(1)}, u32[]{:S(2)}, u32[]{:S(2)}) collective-permute-start(bf16[3,768,256]{2,1,0:T(8,128)(2,1)S(1)} %join_ffn.1.refs_4_), channel_id=1, source_target_pairs={{0,16},{16,0},{1,17},{17,1},{2,18},{18,2},{3,19},{19,3},{4,20},{20... | collective-permute-start | bytes 3538952 | tf_op jit(solution)/shard_map/ppermute | solution.py:627
  96.4 27.6 %collective-permute-start.19 = (bf16[256,1536]{1,0:T(8,128)(2,1)}, bf16[256,1536]{1,0:T(8,128)(2,1)S(1)}, u32[]{:S(2)}, u32[]{:S(2)}) collective-permute-start(bf16[256,1536]{1,0:T(8,128)(2,1)} %refs_4_), channel_id=1, source_target_pairs={{0,4},{4,0},{1,5},{5,1},{2,6},{6,2},{3,7},{7,3},{8,12},{12,8},{9,1... | collective-permute-start | bytes 2359304 | tf_op jit(solution)/shard_map/ppermute | solution.py:627
  132.9 29.8 %collective-permute-start.25 = (bf16[3,768,256]{2,1,0:T(8,128)(2,1)S(1)}, bf16[3,768,256]{2,1,0:T(8,128)(2,1)S(1)}, u32[]{:S(2)}, u32[]{:S(2)}) collective-permute-start(bf16[3,768,256]{2,1,0:T(8,128)(2,1)S(1)} %copy-done.20), channel_id=1, source_target_pairs={{0,16},{16,0},{1,17},{17,1},{2,18},{18,2},{3,19},{19,3},{4,20},{20... | collective-permute-start | bytes 3538952 | tf_op jit(solution)/shard_map/ppermute | solution.py:627
  134.4 28.2 %collective-permute-start.24 = (bf16[2,768,256]{2,1,0:T(8,128)(2,1)}, bf16[2,768,256]{2,1,0:T(8,128)(2,1)S(1)}, u32[]{:S(2)}, u32[]{:S(2)}) collective-permute-start(bf16[2,768,256]{2,1,0:T(8,128)(2,1)} %pad_maximum_fusion.2), channel_id=1, source_target_pairs={{0,1},{1,0},{2,3},{3,2},{4,5},{5,4},{6,7},{7,6},{8,9},{9,8},{10,11... | collective-permute-start | bytes 2359304 | tf_op jit(solution)/shard_map/ppermute | solution.py:631
  134.5 28.1 %collective-permute-start.23 = (bf16[768,256]{1,0:T(8,128)(2,1)S(1)}, bf16[768,256]{1,0:T(8,128)(2,1)}, u32[]{:S(2)}, u32[]{:S(2)}) collective-permute-start(bf16[768,256]{1,0:T(8,128)(2,1)S(1)} %copy-done.111), channel_id=1, source_target_pairs={{0,3},{1,2},{2,1},{3,0},{4,7},{5,6},{6,5},{7,4},{8,11},{9,10},{10,... | collective-permute-start | bytes 1179656 | tf_op jit(solution)/shard_map/ppermute | solution.py:631
  164.6 28.7 %all-to-all-start.1 = ((bf16[4,256,384]{2,1,0:T(8,128)(2,1)}), bf16[4,256,384]{2,1,0:T(8,128)(2,1)}, u32[]{:S(2)}, u32[]{:S(2)}) async-start(bf16[4,256,384]{2,1,0:T(8,128)(2,1)} %copy-done.34), calls=%async_computation.1 | async-start | bytes 1572864 | tf_op jit(solution)/shard_map/all_to_all | solution.py:652
  169.0 23.4 %collective-permute-start.26 = (bf16[2,768,256]{2,1,0:T(8,128)(2,1)}, bf16[2,768,256]{2,1,0:T(8,128)(2,1)S(1)}, u32[]{:S(2)}, u32[]{:S(2)}) collective-permute-start(bf16[2,768,256]{2,1,0:T(8,128)(2,1)} %copy-done.73), channel_id=1, source_target_pairs={{0,16},{16,0},{1,17},{17,1},{2,18},{18,2},{3,19},{19,3},{4,20},{20... | collective-permute-start | bytes 2359304 | tf_op jit(solution)/shard_map/ppermute | solution.py:627
  169.5 22.8 %collective-permute-start.27 = (bf16[768,256]{1,0:T(8,128)(2,1)}, bf16[768,256]{1,0:T(8,128)(2,1)}, u32[]{:S(2)}, u32[]{:S(2)}) collective-permute-start(bf16[768,256]{1,0:T(8,128)(2,1)} %get-tuple-element.292), channel_id=1, source_target_pairs={{0,1},{1,0},{2,3},{3,2},{4,5},{5,4},{6,7},{7,6},{8,9},{9,8},{10,11... | collective-permute-start | bytes 1179656 | tf_op jit(solution)/shard_map/ppermute | solution.py:631
  201.4 20.2 %collective-permute-start.30 = (bf16[2,768,256]{2,1,0:T(8,128)(2,1)S(1)}, bf16[2,768,256]{2,1,0:T(8,128)(2,1)S(1)}, u32[]{:S(2)}, u32[]{:S(2)}) collective-permute-start(bf16[2,768,256]{2,1,0:T(8,128)(2,1)S(1)} %copy-done.108), channel_id=1, source_target_pairs={{0,1},{1,0},{2,3},{3,2},{4,5},{5,4},{6,7},{7,6},{8,9},{9,8},{10,11... | collective-permute-start | bytes 2359304 | tf_op jit(solution)/shard_map/ppermute | solution.py:631
  309.3 28.7 %collective-permute-start.43 = (bf16[3,768,256]{2,1,0:T(8,128)(2,1)}, bf16[3,768,256]{2,1,0:T(8,128)(2,1)}, u32[]{:S(2)}, u32[]{:S(2)}) collective-permute-start(bf16[3,768,256]{2,1,0:T(8,128)(2,1)} %get-tuple-element.361), channel_id=1, source_target_pairs={{0,16},{16,0},{1,17},{17,1},{2,18},{18,2},{3,19},{19,3},{4,20},{20... | collective-permute-start | bytes 3538952 | tf_op jit(solution)/shard_map/ppermute | solution.py:627
  318.0 25.0 %all-to-all-start.2 = ((bf16[4,256,384]{2,1,0:T(8,128)(2,1)}), bf16[4,256,384]{2,1,0:T(8,128)(2,1)S(1)}, u32[]{:S(2)}, u32[]{:S(2)}) async-start(bf16[4,256,384]{2,1,0:T(8,128)(2,1)} %copy-done.35), calls=%async_computation.2 | async-start | bytes 1572864 | tf_op jit(solution)/shard_map/all_to_all | solution.py:652
  342.9 41.1 %collective-permute-start.46 = (bf16[4,96,768]{2,1,0:T(8,128)(2,1)}, bf16[4,96,768]{2,1,0:T(8,128)(2,1)S(1)}, u32[]{:S(2)}, u32[]{:S(2)}) collective-permute-start(bf16[4,96,768]{2,1,0:T(8,128)(2,1)} %copy-done.77), channel_id=1, source_target_pairs={{0,16},{16,0},{1,17},{17,1},{2,18},{18,2},{3,19},{19,3},{4,20},{20... | collective-permute-start | bytes 1769480 | tf_op jit(solution)/shard_map/ppermute | solution.py:627
  343.4 40.8 %collective-permute-start.44 = (bf16[3,768,256]{2,1,0:T(8,128)(2,1)}, bf16[3,768,256]{2,1,0:T(8,128)(2,1)S(1)}, u32[]{:S(2)}, u32[]{:S(2)}) collective-permute-start(bf16[3,768,256]{2,1,0:T(8,128)(2,1)} %add_convert_fusion.5), channel_id=1, source_target_pairs={{0,1},{1,0},{2,3},{3,2},{4,5},{5,4},{6,7},{7,6},{8,9},{9,8},{10,11... | collective-permute-start | bytes 3538952 | tf_op jit(solution)/shard_map/ppermute | solution.py:631
  343.4 40.8 %collective-permute-start.45 = (bf16[3,768,256]{2,1,0:T(8,128)(2,1)}, bf16[3,768,256]{2,1,0:T(8,128)(2,1)S(1)}, u32[]{:S(2)}, u32[]{:S(2)}) collective-permute-start(bf16[3,768,256]{2,1,0:T(8,128)(2,1)} %get-tuple-element.375), channel_id=1, source_target_pairs={{0,16},{16,0},{1,17},{17,1},{2,18},{18,2},{3,19},{19,3},{4,20},{20... | collective-permute-start | bytes 3538952 | tf_op jit(solution)/shard_map/ppermute | solution.py:627
  389.9 42.1 %all-to-all-start.3 = ((bf16[4,256,768]{2,1,0:T(8,128)(2,1)}), bf16[4,256,768]{2,1,0:T(8,128)(2,1)}, u32[]{:S(2)}, u32[]{:S(2)}) async-start(bf16[4,256,768]{2,1,0:T(8,128)(2,1)} %pack.1), calls=%async_computation.3 | async-start | bytes 3145728 | tf_op jit(solution)/shard_map/all_to_all | solution.py:652
  394.6 28.3 %collective-permute-start.51 = (bf16[3,768,256]{2,1,0:T(8,128)(2,1)}, bf16[3,768,256]{2,1,0:T(8,128)(2,1)S(1)}, u32[]{:S(2)}, u32[]{:S(2)}) collective-permute-start(bf16[3,768,256]{2,1,0:T(8,128)(2,1)} %get-tuple-element.399), channel_id=1, source_target_pairs={{0,16},{16,0},{1,17},{17,1},{2,18},{18,2},{3,19},{19,3},{4,20},{20... | collective-permute-start | bytes 3538952 | tf_op jit(solution)/shard_map/ppermute | solution.py:627
  395.1 29.1 %collective-permute-start.48 = (bf16[256,1536]{1,0:T(8,128)(2,1)}, bf16[256,1536]{1,0:T(8,128)(2,1)S(1)}, u32[]{:S(2)}, u32[]{:S(2)}) collective-permute-start(bf16[256,1536]{1,0:T(8,128)(2,1)} %copy-done.72), channel_id=1, source_target_pairs={{0,4},{4,0},{1,5},{5,1},{2,6},{6,2},{3,7},{7,3},{8,12},{12,8},{9,1... | collective-permute-start | bytes 2359304 | tf_op jit(solution)/shard_map/ppermute | solution.py:627
  396.6 27.6 %collective-permute-start.50 = (bf16[256,1536]{1,0:T(8,128)(2,1)S(1)}, bf16[256,1536]{1,0:T(8,128)(2,1)S(1)}, u32[]{:S(2)}, u32[]{:S(2)}) collective-permute-start(bf16[256,1536]{1,0:T(8,128)(2,1)S(1)} %add_convert_fusion.6), channel_id=1, source_target_pairs={{0,8},{8,0},{1,9},{9,1},{2,10},{10,2},{3,11},{11,3},{4,12},{12,4},... | collective-permute-start | bytes 2359304 | tf_op jit(solution)/shard_map/ppermute | solution.py:627
  441.8 28.7 %collective-permute-start.53 = (bf16[2,192,768]{2,1,0:T(8,128)(2,1)}, bf16[2,192,768]{2,1,0:T(8,128)(2,1)}, u32[]{:S(2)}, u32[]{:S(2)}) collective-permute-start(bf16[2,192,768]{2,1,0:T(8,128)(2,1)} %get-tuple-element.407), channel_id=1, source_target_pairs={{0,16},{16,0},{1,17},{17,1},{2,18},{18,2},{3,19},{19,3},{4,20},{20... | collective-permute-start | bytes 1769480 | tf_op jit(solution)/shard_map/ppermute | solution.py:627
  443.3 44.1 %collective-permute-start.55 = (bf16[3,768,256]{2,1,0:T(8,128)(2,1)}, bf16[3,768,256]{2,1,0:T(8,128)(2,1)}, u32[]{:S(2)}, u32[]{:S(2)}) collective-permute-start(bf16[3,768,256]{2,1,0:T(8,128)(2,1)} %add_convert_fusion.2), channel_id=1, source_target_pairs={{0,1},{1,0},{2,3},{3,2},{4,5},{5,4},{6,7},{7,6},{8,9},{9,8},{10,11... | collective-permute-start | bytes 3538952 | tf_op jit(solution)/shard_map/ppermute | solution.py:631
  443.3 50.7 %collective-permute-start.56 = (bf16[3,768,256]{2,1,0:T(8,128)(2,1)}, bf16[3,768,256]{2,1,0:T(8,128)(2,1)}, u32[]{:S(2)}, u32[]{:S(2)}) collective-permute-start(bf16[3,768,256]{2,1,0:T(8,128)(2,1)} %get-tuple-element.414), channel_id=1, source_target_pairs={{0,16},{16,0},{1,17},{17,1},{2,18},{18,2},{3,19},{19,3},{4,20},{20... | collective-permute-start | bytes 3538952 | tf_op jit(solution)/shard_map/ppermute | solution.py:627
  443.8 43.6 %collective-permute-start.54 = (bf16[2,768,256]{2,1,0:T(8,128)(2,1)}, bf16[2,768,256]{2,1,0:T(8,128)(2,1)}, u32[]{:S(2)}, u32[]{:S(2)}) collective-permute-start(bf16[2,768,256]{2,1,0:T(8,128)(2,1)} %slice.92), channel_id=1, source_target_pairs={{0,3},{1,2},{2,1},{3,0},{4,7},{5,6},{6,5},{7,4},{8,11},{9,10},{10,... | collective-permute-start | bytes 2359304 | tf_op jit(solution)/shard_map/ppermute | solution.py:631
  500.2 20.6 %collective-permute-start.57 = (bf16[288,768]{1,0:T(8,128)(2,1)}, bf16[288,768]{1,0:T(8,128)(2,1)}, u32[]{:S(2)}, u32[]{:S(2)}) collective-permute-start(bf16[288,768]{1,0:T(8,128)(2,1)} %copy-done.79), channel_id=1, source_target_pairs={{0,1},{1,0},{2,3},{3,2},{4,5},{5,4},{6,7},{7,6},{8,9},{9,8},{10,11... | collective-permute-start | bytes 1327112 | tf_op jit(solution)/shard_map/ppermute | solution.py:631
  500.2 29.8 %collective-permute-start.58 = (bf16[288,768]{1,0:T(8,128)(2,1)}, bf16[288,768]{1,0:T(8,128)(2,1)S(1)}, u32[]{:S(2)}, u32[]{:S(2)}) collective-permute-start(bf16[288,768]{1,0:T(8,128)(2,1)} %copy-done.78), channel_id=1, source_target_pairs={{0,1},{1,0},{2,3},{3,2},{4,5},{5,4},{6,7},{7,6},{8,9},{9,8},{10,11... | collective-permute-start | bytes 1327112 | tf_op jit(solution)/shard_map/ppermute | solution.py:631
  504.2 25.7 %collective-permute-start.60 = (bf16[256,1536]{1,0:T(8,128)(2,1)S(1)}, bf16[256,1536]{1,0:T(8,128)(2,1)S(1)}, u32[]{:S(2)}, u32[]{:S(2)}) collective-permute-start(bf16[256,1536]{1,0:T(8,128)(2,1)S(1)} %fusion.11), channel_id=1, source_target_pairs={{0,8},{8,0},{1,9},{9,1},{2,10},{10,2},{3,11},{11,3},{4,12},{12,4},... | collective-permute-start | bytes 2359304 | tf_op jit(solution)/shard_map/ppermute | solution.py:627
  (167 other events, 1960.9 us)
where the time goes:
time: 583 us; the launch traced here: 575 us
  waiting for transfers between devices  270 us (46%)
  Pallas kernels  134 us (23%)
  starting transfers between devices  84.6 us (15%)
  local copies, waits for them, and re-layouts  44 us (8%)
  other arithmetic  41.1 us (7%)
    ppermute x51, waiting for transfers between devices, swap(): return lax.ppermute(value, axis, [(0, 1), (1, 0)])  183 us
    pallas_call x18, Pallas kernels, run(): pl.pallas_call(kernel, out_shape=[shape(*o) if isinstance(o[0], tuple) el...  80.2 us
    ppermute x20, waiting for transfers between devices, sent(): lax.ppermute(value, axis, [(i, i ^ bits) for i in range(lax.axis_size(axi...  62.9 us
    unnamed x241, local copies, waits for them, and re-layouts  37.8 us
    pallas_call x1, Pallas kernels, attend_back(): pl.pallas_call(functools.partial(attend_back_kernel, block=block, tile=ti...  35 us
    ppermute x51, starting transfers between devices, swap(): return lax.ppermute(value, axis, [(0, 1), (1, 0)])  32.9 us
    ppermute x20, starting transfers between devices, sent(): lax.ppermute(value, axis, [(i, i ^ bits) for i in range(lax.axis_size(axi...  31.2 us
    pallas_call x1, Pallas kernels, attend(): pl.pallas_call(functools.partial(attend_kernel, block=block, tile=tile),...  18.7 us
  transfers between devices with their start and end apart: 79, of which 42 were waited for; matrix products, arithmetic and copies ran while one was open for 6% of the time, Pallas kernels for 18%

commit v1 on v0

--- a/solution.py
+++ b/solution.py
@@ -895,7 +895,7 @@
         (onto_three, onto_one, feed_home, gains, squares, grad_tokens)
     )
     attn_home = spread(part_attn(ids, sums[0], onto_one, onto_three))
-    attn_home, gains, squares = fence((attn_home, gains, squares))
+    attn_home[1], gains, squares = fence((attn_home[1], gains, squares))
     totals = over_z(jnp.concatenate([gains.reshape(-1), squares]))
     grad_gate, grad_up, grad_down = finish_ffn(ids, feed_home, gain_ffn)
     grad_query, grad_key, grad_value, grad_outproj = finish_attn(ids, attn_home, gain_attn)

time: 583 us -> 576 us (0.988)
  waiting for transfers between devices: 270 us -> 263 us
  transfers between devices with their start and end apart: 79 -> 79, of which waited for: 42 -> 40; matrix products, arithmetic and copies ran while one was open for 6% -> 6% of each run, Pallas kernels for 18% -> 19%
where the time goes in v1:
time: 576 us; the launch traced here: 568 us
  waiting for transfers between devices  263 us (46%)
  Pallas kernels  134 us (23%)
  starting transfers between devices  84.6 us (15%)
  local copies, waits for them, and re-layouts  44 us (8%)
  other arithmetic  41.1 us (7%)
    ppermute x51, waiting for transfers between devices, swap(): return lax.ppermute(value, axis, [(0, 1), (1, 0)])  178 us
    pallas_call x18, Pallas kernels, run(): pl.pallas_call(kernel, out_shape=[shape(*o) if isinstance(o[0], tuple) el...  80.2 us
    ppermute x20, waiting for transfers between devices, sent(): lax.ppermute(value, axis, [(i, i ^ bits) for i in range(lax.axis_size(axi...  62.9 us
    unnamed x241, local copies, waits for them, and re-layouts  37.8 us
    pallas_call x1, Pallas kernels, attend_back(): pl.pallas_call(functools.partial(attend_back_kernel, block=block, tile=ti...  35 us
    ppermute x51, starting transfers between devices, swap(): return lax.ppermute(value, axis, [(0, 1), (1, 0)])  32.9 us
    ppermute x20, starting transfers between devices, sent(): lax.ppermute(value, axis, [(i, i ^ bits) for i in range(lax.axis_size(axi...  31.2 us
    pallas_call x1, Pallas kernels, attend(): pl.pallas_call(functools.partial(attend_kernel, block=block, tile=tile),...  18.7 us
  transfers between devices with their start and end apart: 79, of which 40 were waited for; matrix products, arithmetic and copies ran while one was open for 6% of the time, Pallas kernels for 19%

profile of v1, /device:TPU:0, one launch (start us, length us, event | category | flops | bytes accessed | tf_op | source)
XLA Modules:
  0.0 568.4 jit_solution(7081946431229256233)
XLA Ops:
  25.4 8.4 %collective-permute-done.4.refs_2_ = bf16[3,192,256]{2,1,0:T(8,128)(2,1)S(1)} collective-permute-done((bf16[3,192,256]{2,1,0:T(8,128)(2,1)S(1)}, bf16[3,192,256]{2,1,0:T(8,128)(2,1)S(1)}, u32[]{:S(2)}, u32[]{:S(2)}) %collective-permute-start.4) | collective-permute-done | bytes 294944 | tf_op jit(solution)/shard_map/ppermute | solution.py:627
  33.8 4.1 collective-permute-done.5.refs_3_
  47.9 16.3 %collective-permute-done.13.refs_2_.refs_3_ = bf16[256,1536]{1,0:T(8,128)(2,1)S(1)} collective-permute-done((bf16[256,1536]{1,0:T(8,128)(2,1)S(1)}, bf16[256,1536]{1,0:T(8,128)(2,1)S(1)}, u32[]{:S(2)}, u32[]{:S(2)}) %collective-permute-start.13) | collective-permute-done | bytes 786464 | tf_op jit(solution)/shard_map/ppermute | solution.py:627
  71.4 8.6 %collective-permute-done.15.refs_9_.refs_5_.refs_10_ = bf16[288,768]{1,0:T(8,128)(2,1)S(1)} collective-permute-done((bf16[288,768]{1,0:T(8,128)(2,1)S(1)}, bf16[288,768]{1,0:T(8,128)(2,1)S(1)}, u32[]{:S(2)}, u32[]{:S(2)}) %collective-permute-start.15) | collective-permute-done | bytes 442400 | tf_op jit(solution)/shard_map/ppermute | solution.py:627
  80.0 5.1 project.1
  89.5 4.8 all-to-all-start
  96.4 17.3 %collective-permute-done.20.refs_2_.refs_6_ = bf16[256,1536]{1,0:T(8,128)(2,1)S(1)} collective-permute-done((bf16[256,1536]{1,0:T(8,128)(2,1)}, bf16[256,1536]{1,0:T(8,128)(2,1)S(1)}, u32[]{:S(2)}, u32[]{:S(2)}) %collective-permute-start.20) | collective-permute-done | bytes 786464 | tf_op jit(solution)/shard_map/ppermute | solution.py:627
  126.8 4.6 all-to-all-done.own
  135.9 18.7 %attend.1 = (bf16[4,256,384]{2,1,0:T(8,128)(2,1)S(1)}, bf16[4096,128]{1,0:T(8,128)(2,1)S(1)}, bf16[2,4096,128]{2,1,0:T(8,128)(2,1)S(1)}, bf16[4096,128]{1,0:T(8,128)(2,1)S(1)}, f32[8,4096]{1,0:T(8,128)S(1)}) custom-call(s32[3]{0:T(128)S(1)} %pad_add_fusion.ids, bf16[4,256,768]{2,1,0:T(8,128)(2,1)} %all-to-all-done.own, ...), custom_call_target="tpu_custom_call" | custom-call | flops 20999999488 | bytes 1 | tf_op jit(solution)/shard_map/attend/pallas_call | solution.py:112
  164.6 4.4 all-to-all-start.1
  173.6 18.7 %collective-permute-done.27.refs_8_ = bf16[768,256]{1,0:T(8,128)(2,1)} collective-permute-done((bf16[768,256]{1,0:T(8,128)(2,1)}, bf16[768,256]{1,0:T(8,128)(2,1)}, u32[]{:S(2)}, u32[]{:S(2)}) %collective-permute-start.27) | collective-permute-done | bytes 393248 | tf_op jit(solution)/shard_map/ppermute | solution.py:631
  203.8 16.3 %collective-permute-done.29 = bf16[256,1536]{1,0:T(8,128)(2,1)S(1)} collective-permute-done((bf16[256,1536]{1,0:T(8,128)(2,1)S(1)}, bf16[256,1536]{1,0:T(8,128)(2,1)S(1)}, u32[]{:S(2)}, u32[]{:S(2)}) %collective-permute-start.29) | collective-permute-done | bytes 786464 | tf_op jit(solution)/shard_map/ppermute | solution.py:627
  222.7 17.7 %collective-permute-done.34.refs_0_.refs_2_ = bf16[256,1536]{1,0:T(8,128)(2,1)S(1)} collective-permute-done((bf16[256,1536]{1,0:T(8,128)(2,1)S(1)}, bf16[256,1536]{1,0:T(8,128)(2,1)S(1)}, u32[]{:S(2)}, u32[]{:S(2)}) %collective-permute-start.34) | collective-permute-done | bytes 786464 | tf_op jit(solution)/shard_map/ppermute | solution.py:627
  242.8 15.6 %feed.2 = (bf16[256,1536]{1,0:T(8,128)(2,1)S(1)}, bf16[256,1536]{1,0:T(8,128)(2,1)}, bf16[256,1536]{1,0:T(8,128)(2,1)S(1)}, bf16[256,1536]{1,0:T(8,128)(2,1)S(1)...) custom-call(s32[3]{0:T(128)S(1)} %pad_add_fusion.ids, ...), custom_call_target="tpu_custom_call" | custom-call | flops 18000001024 | bytes 1 | tf_op jit(solution)/shard_map/feed/pallas_call | solution.py:229
  263.6 15.2 %feed.3 = (bf16[256,1536]{1,0:T(8,128)(2,1)S(1)}, bf16[256,1536]{1,0:T(8,128)(2,1)S(1)}, bf16[256,1536]{1,0:T(8,128)(2,1)S(1)}, bf16[256,1536]{1,0:T(8,128)(2,1)...) custom-call(s32[3]{0:T(128)S(1)} %pad_add_fusion.ids, ...), custom_call_target="tpu_custom_call" | custom-call | flops 18000001024 | bytes 1 | tf_op jit(solution)/shard_map/feed/pallas_call | solution.py:229
  290.7 14.5 %feed_weights.1 = (bf16[3,768,256]{2,1,0:T(8,128)(2,1)S(1)}, bf16[3,768,256]{2,1,0:T(8,128)(2,1)}, bf16[3,768,256]{2,1,0:T(8,128)(2,1)}, bf16[3,768,256]{2,1,0:T...) custom-call(s32[3]{0:T(128)S(1)} %pad_add_fusion.ids, ...), custom_call_target="tpu_custom_call" | custom-call | flops 17000000512 | bytes 1 | tf_op jit(solution)/shard_map/feed_weights/pallas_call | solution.py:229
  305.3 4.1 collective-permute-done.40.refs_2_
  318.0 4.6 all-to-all-start.2
  322.6 15.5 %collective-permute-done.43 = bf16[3,768,256]{2,1,0:T(8,128)(2,1)} collective-permute-done((bf16[3,768,256]{2,1,0:T(8,128)(2,1)}, bf16[3,768,256]{2,1,0:T(8,128)(2,1)}, u32[]{:S(2)}, u32[]{:S(2)}) %collective-permute-start.43) | collective-permute-done | bytes 1179680 | tf_op jit(solution)/shard_map/ppermute | solution.py:627
  349.0 35.0 %attend_back.1 = (bf16[4,256,384]{2,1,0:T(8,128)(2,1)S(1)}, bf16[4096,128]{1,0:T(8,128)(2,1)S(1)}, bf16[4096,128]{1,0:T(8,128)(2,1)S(1)}) custom-call(s32[3]{0:T(128)S(1)} %pad_add_fusion.ids, bf16[4096,128]{1,0:T(8,128)(2,1)S(1)} %copy-done.87, bf16[2,4096,128]{2,1,0:T(8,128)(2,1)S(1)} %copy-done.85, bf16[4096,128]{1,0:T(8,128)(2,1)S(1)} %copy-done.89, ...), custom_call_target="tpu_custom_call" | custom-call | flops 38999998464 | bytes 1 | tf_op jit(solution)/shard_map/attend_back/pallas_call | solution.py:201
  389.9 4.6 all-to-all-start.3
  401.5 21.4 %collective-permute-done.51 = bf16[3,768,256]{2,1,0:T(8,128)(2,1)S(1)} collective-permute-done((bf16[3,768,256]{2,1,0:T(8,128)(2,1)}, bf16[3,768,256]{2,1,0:T(8,128)(2,1)S(1)}, u32[]{:S(2)}, u32[]{:S(2)}) %collective-permute-start.51) | collective-permute-done | bytes 1179680 | tf_op jit(solution)/shard_map/ppermute | solution.py:627
  435.4 5.8 %project_weights.1 = (bf16[1024,768]{1,0:T(8,128)(2,1)S(1)}, bf16[2,192,768]{2,1,0:T(8,128)(2,1)S(1)}, bf16[2,192,768]{2,1,0:T(8,128)(2,1)S(1)}, bf16[2,192,768]{2,1,0:T(8,128)(2,1)}, bf16[2,192,768]{2,1,0:T(8,128)(2,1)}) custom-call(s32[3]{0:T(128)S(1)} %pad_add_fusion.ids, bf16[4,256,768]{2,1,0:T(8,128)(2,1)} %all-to-all-done.3.refs_0_, ...), custom_call_target="tpu_custom_call" | custom-call | flops 99999997952 | bytes 1 | tf_op jit(solution)/shard_map/project_weights/pallas_call | solution.py:229
  451.5 6.3 %collective-permute-done.52.refs_1_ = bf16[2,192,768]{2,1,0:T(8,128)(2,1)} collective-permute-done((bf16[2,192,768]{2,1,0:T(8,128)(2,1)}, bf16[2,192,768]{2,1,0:T(8,128)(2,1)}, u32[]{:S(2)}, u32[]{:S(2)}) %collective-permute-start.52) | collective-permute-done | bytes 589856 | tf_op jit(solution)/shard_map/ppermute | solution.py:627
  457.9 12.6 %collective-permute-done.53.refs_3_ = bf16[2,192,768]{2,1,0:T(8,128)(2,1)} collective-permute-done((bf16[2,192,768]{2,1,0:T(8,128)(2,1)}, bf16[2,192,768]{2,1,0:T(8,128)(2,1)}, u32[]{:S(2)}, u32[]{:S(2)}) %collective-permute-start.53) | collective-permute-done | bytes 589856 | tf_op jit(solution)/shard_map/ppermute | solution.py:627
  477.3 10.1 %collective-permute-done.54 = bf16[2,768,256]{2,1,0:T(8,128)(2,1)} collective-permute-done((bf16[2,768,256]{2,1,0:T(8,128)(2,1)}, bf16[2,768,256]{2,1,0:T(8,128)(2,1)}, u32[]{:S(2)}, u32[]{:S(2)}) %collective-permute-start.54) | collective-permute-done | bytes 786464 | tf_op jit(solution)/shard_map/ppermute | solution.py:631
  487.4 6.6 %collective-permute-done.56 = bf16[3,768,256]{2,1,0:T(8,128)(2,1)} collective-permute-done((bf16[3,768,256]{2,1,0:T(8,128)(2,1)}, bf16[3,768,256]{2,1,0:T(8,128)(2,1)}, u32[]{:S(2)}, u32[]{:S(2)}) %collective-permute-start.56) | collective-permute-done | bytes 1179680 | tf_op jit(solution)/shard_map/ppermute | solution.py:627
  505.5 6.7 %collective-permute-done.61 = bf16[1,768,256]{2,1,0:T(8,128)(2,1)} collective-permute-done((bf16[1,768,256]{2,1,0:T(8,128)(2,1)}, bf16[1,768,256]{2,1,0:T(8,128)(2,1)}, u32[]{:S(2)}, u32[]{:S(2)}) %collective-permute-start.61) | collective-permute-done | bytes 393248 | tf_op jit(solution)/shard_map/ppermute | solution.py:631
  514.8 6.0 %collective-permute-done.57 = bf16[288,768]{1,0:T(8,128)(2,1)} collective-permute-done((bf16[288,768]{1,0:T(8,128)(2,1)}, bf16[288,768]{1,0:T(8,128)(2,1)}, u32[]{:S(2)}, u32[]{:S(2)}) %collective-permute-start.57) | collective-permute-done | bytes 442400 | tf_op jit(solution)/shard_map/ppermute | solution.py:631
  521.9 8.1 %collective-permute-done.58.one = bf16[288,768]{1,0:T(8,128)(2,1)S(1)} collective-permute-done((bf16[288,768]{1,0:T(8,128)(2,1)}, bf16[288,768]{1,0:T(8,128)(2,1)S(1)}, u32[]{:S(2)}, u32[]{:S(2)}) %collective-permute-start.58) | collective-permute-done | bytes 442400 | tf_op jit(solution)/shard_map/ppermute | solution.py:631
  543.2 5.5 collective-permute-done.67.refs_3_
  552.2 7.9 %collective-permute-start.72 = (f32[387]{0:T(512)S(1)}, f32[387]{0:T(512)S(1)}, u32[]{:S(2)}, u32[]{:S(2)}) collective-permute-start(f32[387]{0:T(512)S(1)} %constant_dynamic-update-slice_fusion), channel_id=1, source_target_pairs={{0,1},{1,0},{2,3},{3,2},{4,5},{5,4},{6,7},{7,6},{8,9},{9,8},{10,11... | collective-permute-start | bytes 4652 | tf_op jit(solution)/shard_map/ppermute | solution.py:631
  (461 shorter events, 215.2 us)
Async XLA Ops:
  22.4 20.2 %collective-permute-start.7 = (bf16[288,768]{1,0:T(8,128)(2,1)S(1)}, bf16[288,768]{1,0:T(8,128)(2,1)S(1)}, u32[]{:S(2)}, u32[]{:S(2)}) collective-permute-start(bf16[288,768]{1,0:T(8,128)(2,1)S(1)} %join_attn.1.refs_4_.refs_0_.refs_5_), channel_id=1, source_target_pairs={{0,1},{1,0},{2,3},{3,2},{4,5},{5,4},{6,7},{7,6},{8,9},{9,8},{10,11... | collective-permute-start | bytes 1327112 | tf_op jit(solution)/shard_map/ppermute | solution.py:631
  22.4 20.2 %collective-permute-start.8 = (bf16[288,768]{1,0:T(8,128)(2,1)S(1)}, bf16[288,768]{1,0:T(8,128)(2,1)S(1)}, u32[]{:S(2)}, u32[]{:S(2)}) collective-permute-start(bf16[288,768]{1,0:T(8,128)(2,1)S(1)} %join_attn.1.refs_4_.refs_0_.refs_5_), channel_id=1, source_target_pairs={{0,16},{16,0},{1,17},{17,1},{2,18},{18,2},{3,19},{19,3},{4,20},{20... | collective-permute-start | bytes 1327112 | tf_op jit(solution)/shard_map/ppermute | solution.py:627
  42.7 24.0 %collective-permute-start.10 = (bf16[2,288,768]{2,1,0:T(8,128)(2,1)S(1)}, bf16[2,288,768]{2,1,0:T(8,128)(2,1)S(1)}, u32[]{:S(2)}, u32[]{:S(2)}) collective-permute-start(bf16[2,288,768]{2,1,0:T(8,128)(2,1)S(1)} %pad_maximum_fusion.1.refs_6_.refs_2_.refs_7_), channel_id=1, source_target_pairs={{0,16},{16,0},{1,17},{17,1},{2,18},{18,2},{3,19},{19,3},{4,20},{20... | collective-permute-start | bytes 2654216 | tf_op jit(solution)/shard_map/ppermute | solution.py:627
  44.2 20.0 %collective-permute-start.13 = (bf16[256,1536]{1,0:T(8,128)(2,1)S(1)}, bf16[256,1536]{1,0:T(8,128)(2,1)S(1)}, u32[]{:S(2)}, u32[]{:S(2)}) collective-permute-start(bf16[256,1536]{1,0:T(8,128)(2,1)S(1)} %fusion.1.refs_0_.refs_1_), channel_id=1, source_target_pairs={{0,8},{8,0},{1,9},{9,1},{2,10},{10,2},{3,11},{11,3},{4,12},{12,4},... | collective-permute-start | bytes 2359304 | tf_op jit(solution)/shard_map/ppermute | solution.py:627
  45.7 20.9 %collective-permute-start.9 = (bf16[288,768]{1,0:T(8,128)(2,1)S(1)}, bf16[288,768]{1,0:T(8,128)(2,1)S(1)}, u32[]{:S(2)}, u32[]{:S(2)}) collective-permute-start(bf16[288,768]{1,0:T(8,128)(2,1)S(1)} %collective-permute-done.6), channel_id=1, source_target_pairs={{0,1},{1,0},{2,3},{3,2},{4,5},{5,4},{6,7},{7,6},{8,9},{9,8},{10,11... | collective-permute-start | bytes 1327112 | tf_op jit(solution)/shard_map/ppermute | solution.py:631
  68.6 20.8 %collective-permute-start.17 = (bf16[768,256]{1,0:T(8,128)(2,1)S(1)}, bf16[768,256]{1,0:T(8,128)(2,1)}, u32[]{:S(2)}, u32[]{:S(2)}) collective-permute-start(bf16[768,256]{1,0:T(8,128)(2,1)S(1)} %get-tuple-element.479), channel_id=1, source_target_pairs={{0,3},{1,2},{2,1},{3,0},{4,7},{5,6},{6,5},{7,4},{8,11},{9,10},{10,... | collective-permute-start | bytes 1179656 | tf_op jit(solution)/shard_map/ppermute | solution.py:631
  89.5 41.9 %all-to-all-start = ((bf16[4,256,768]{2,1,0:T(8,128)(2,1)}), bf16[4,256,768]{2,1,0:T(8,128)(2,1)}, u32[]{:S(2)}, u32[]{:S(2)}) async-start(bf16[4,256,768]{2,1,0:T(8,128)(2,1)} %copy-done), calls=%async_computation | async-start | bytes 3145728 | tf_op jit(solution)/shard_map/all_to_all | solution.py:652
  94.9 30.0 %collective-permute-start.18 = (bf16[3,768,256]{2,1,0:T(8,128)(2,1)S(1)}, bf16[3,768,256]{2,1,0:T(8,128)(2,1)S(1)}, u32[]{:S(2)}, u32[]{:S(2)}) collective-permute-start(bf16[3,768,256]{2,1,0:T(8,128)(2,1)S(1)} %join_ffn.1.refs_4_), channel_id=1, source_target_pairs={{0,16},{16,0},{1,17},{17,1},{2,18},{18,2},{3,19},{19,3},{4,20},{20... | collective-permute-start | bytes 3538952 | tf_op jit(solution)/shard_map/ppermute | solution.py:627
  96.4 27.6 %collective-permute-start.19 = (bf16[256,1536]{1,0:T(8,128)(2,1)}, bf16[256,1536]{1,0:T(8,128)(2,1)S(1)}, u32[]{:S(2)}, u32[]{:S(2)}) collective-permute-start(bf16[256,1536]{1,0:T(8,128)(2,1)} %refs_4_), channel_id=1, source_target_pairs={{0,4},{4,0},{1,5},{5,1},{2,6},{6,2},{3,7},{7,3},{8,12},{12,8},{9,1... | collective-permute-start | bytes 2359304 | tf_op jit(solution)/shard_map/ppermute | solution.py:627
  132.9 29.8 %collective-permute-start.25 = (bf16[3,768,256]{2,1,0:T(8,128)(2,1)S(1)}, bf16[3,768,256]{2,1,0:T(8,128)(2,1)S(1)}, u32[]{:S(2)}, u32[]{:S(2)}) collective-permute-start(bf16[3,768,256]{2,1,0:T(8,128)(2,1)S(1)} %copy-done.20), channel_id=1, source_target_pairs={{0,16},{16,0},{1,17},{17,1},{2,18},{18,2},{3,19},{19,3},{4,20},{20... | collective-permute-start | bytes 3538952 | tf_op jit(solution)/shard_map/ppermute | solution.py:627
  134.4 28.2 %collective-permute-start.24 = (bf16[2,768,256]{2,1,0:T(8,128)(2,1)}, bf16[2,768,256]{2,1,0:T(8,128)(2,1)S(1)}, u32[]{:S(2)}, u32[]{:S(2)}) collective-permute-start(bf16[2,768,256]{2,1,0:T(8,128)(2,1)} %pad_maximum_fusion.2), channel_id=1, source_target_pairs={{0,1},{1,0},{2,3},{3,2},{4,5},{5,4},{6,7},{7,6},{8,9},{9,8},{10,11... | collective-permute-start | bytes 2359304 | tf_op jit(solution)/shard_map/ppermute | solution.py:631
  134.5 28.1 %collective-permute-start.23 = (bf16[768,256]{1,0:T(8,128)(2,1)S(1)}, bf16[768,256]{1,0:T(8,128)(2,1)}, u32[]{:S(2)}, u32[]{:S(2)}) collective-permute-start(bf16[768,256]{1,0:T(8,128)(2,1)S(1)} %copy-done.111), channel_id=1, source_target_pairs={{0,3},{1,2},{2,1},{3,0},{4,7},{5,6},{6,5},{7,4},{8,11},{9,10},{10,... | collective-permute-start | bytes 1179656 | tf_op jit(solution)/shard_map/ppermute | solution.py:631
  164.6 28.7 %all-to-all-start.1 = ((bf16[4,256,384]{2,1,0:T(8,128)(2,1)}), bf16[4,256,384]{2,1,0:T(8,128)(2,1)}, u32[]{:S(2)}, u32[]{:S(2)}) async-start(bf16[4,256,384]{2,1,0:T(8,128)(2,1)} %copy-done.34), calls=%async_computation.1 | async-start | bytes 1572864 | tf_op jit(solution)/shard_map/all_to_all | solution.py:652
  169.0 23.4 %collective-permute-start.26 = (bf16[2,768,256]{2,1,0:T(8,128)(2,1)}, bf16[2,768,256]{2,1,0:T(8,128)(2,1)S(1)}, u32[]{:S(2)}, u32[]{:S(2)}) collective-permute-start(bf16[2,768,256]{2,1,0:T(8,128)(2,1)} %copy-done.73), channel_id=1, source_target_pairs={{0,16},{16,0},{1,17},{17,1},{2,18},{18,2},{3,19},{19,3},{4,20},{20... | collective-permute-start | bytes 2359304 | tf_op jit(solution)/shard_map/ppermute | solution.py:627
  169.5 22.8 %collective-permute-start.27 = (bf16[768,256]{1,0:T(8,128)(2,1)}, bf16[768,256]{1,0:T(8,128)(2,1)}, u32[]{:S(2)}, u32[]{:S(2)}) collective-permute-start(bf16[768,256]{1,0:T(8,128)(2,1)} %get-tuple-element.289), channel_id=1, source_target_pairs={{0,1},{1,0},{2,3},{3,2},{4,5},{5,4},{6,7},{7,6},{8,9},{9,8},{10,11... | collective-permute-start | bytes 1179656 | tf_op jit(solution)/shard_map/ppermute | solution.py:631
  201.4 20.2 %collective-permute-start.30 = (bf16[2,768,256]{2,1,0:T(8,128)(2,1)S(1)}, bf16[2,768,256]{2,1,0:T(8,128)(2,1)S(1)}, u32[]{:S(2)}, u32[]{:S(2)}) collective-permute-start(bf16[2,768,256]{2,1,0:T(8,128)(2,1)S(1)} %copy-done.108), channel_id=1, source_target_pairs={{0,1},{1,0},{2,3},{3,2},{4,5},{5,4},{6,7},{7,6},{8,9},{9,8},{10,11... | collective-permute-start | bytes 2359304 | tf_op jit(solution)/shard_map/ppermute | solution.py:631
  309.3 28.7 %collective-permute-start.43 = (bf16[3,768,256]{2,1,0:T(8,128)(2,1)}, bf16[3,768,256]{2,1,0:T(8,128)(2,1)}, u32[]{:S(2)}, u32[]{:S(2)}) collective-permute-start(bf16[3,768,256]{2,1,0:T(8,128)(2,1)} %get-tuple-element.358), channel_id=1, source_target_pairs={{0,16},{16,0},{1,17},{17,1},{2,18},{18,2},{3,19},{19,3},{4,20},{20... | collective-permute-start | bytes 3538952 | tf_op jit(solution)/shard_map/ppermute | solution.py:627
  318.0 25.0 %all-to-all-start.2 = ((bf16[4,256,384]{2,1,0:T(8,128)(2,1)}), bf16[4,256,384]{2,1,0:T(8,128)(2,1)S(1)}, u32[]{:S(2)}, u32[]{:S(2)}) async-start(bf16[4,256,384]{2,1,0:T(8,128)(2,1)} %copy-done.35), calls=%async_computation.2 | async-start | bytes 1572864 | tf_op jit(solution)/shard_map/all_to_all | solution.py:652
  342.9 41.1 %collective-permute-start.46 = (bf16[4,96,768]{2,1,0:T(8,128)(2,1)}, bf16[4,96,768]{2,1,0:T(8,128)(2,1)S(1)}, u32[]{:S(2)}, u32[]{:S(2)}) collective-permute-start(bf16[4,96,768]{2,1,0:T(8,128)(2,1)} %copy-done.77), channel_id=1, source_target_pairs={{0,16},{16,0},{1,17},{17,1},{2,18},{18,2},{3,19},{19,3},{4,20},{20... | collective-permute-start | bytes 1769480 | tf_op jit(solution)/shard_map/ppermute | solution.py:627
  343.4 40.8 %collective-permute-start.44 = (bf16[3,768,256]{2,1,0:T(8,128)(2,1)}, bf16[3,768,256]{2,1,0:T(8,128)(2,1)S(1)}, u32[]{:S(2)}, u32[]{:S(2)}) collective-permute-start(bf16[3,768,256]{2,1,0:T(8,128)(2,1)} %add_convert_fusion.5), channel_id=1, source_target_pairs={{0,1},{1,0},{2,3},{3,2},{4,5},{5,4},{6,7},{7,6},{8,9},{9,8},{10,11... | collective-permute-start | bytes 3538952 | tf_op jit(solution)/shard_map/ppermute | solution.py:631
  343.4 40.8 %collective-permute-start.45 = (bf16[3,768,256]{2,1,0:T(8,128)(2,1)}, bf16[3,768,256]{2,1,0:T(8,128)(2,1)S(1)}, u32[]{:S(2)}, u32[]{:S(2)}) collective-permute-start(bf16[3,768,256]{2,1,0:T(8,128)(2,1)} %get-tuple-element.372), channel_id=1, source_target_pairs={{0,16},{16,0},{1,17},{17,1},{2,18},{18,2},{3,19},{19,3},{4,20},{20... | collective-permute-start | bytes 3538952 | tf_op jit(solution)/shard_map/ppermute | solution.py:627
  389.9 42.1 %all-to-all-start.3 = ((bf16[4,256,768]{2,1,0:T(8,128)(2,1)}), bf16[4,256,768]{2,1,0:T(8,128)(2,1)}, u32[]{:S(2)}, u32[]{:S(2)}) async-start(bf16[4,256,768]{2,1,0:T(8,128)(2,1)} %pack.1), calls=%async_computation.3 | async-start | bytes 3145728 | tf_op jit(solution)/shard_map/all_to_all | solution.py:652
  394.6 28.3 %collective-permute-start.51 = (bf16[3,768,256]{2,1,0:T(8,128)(2,1)}, bf16[3,768,256]{2,1,0:T(8,128)(2,1)S(1)}, u32[]{:S(2)}, u32[]{:S(2)}) collective-permute-start(bf16[3,768,256]{2,1,0:T(8,128)(2,1)} %get-tuple-element.396), channel_id=1, source_target_pairs={{0,16},{16,0},{1,17},{17,1},{2,18},{18,2},{3,19},{19,3},{4,20},{20... | collective-permute-start | bytes 3538952 | tf_op jit(solution)/shard_map/ppermute | solution.py:627
  395.1 29.1 %collective-permute-start.48 = (bf16[256,1536]{1,0:T(8,128)(2,1)}, bf16[256,1536]{1,0:T(8,128)(2,1)S(1)}, u32[]{:S(2)}, u32[]{:S(2)}) collective-permute-start(bf16[256,1536]{1,0:T(8,128)(2,1)} %copy-done.72), channel_id=1, source_target_pairs={{0,4},{4,0},{1,5},{5,1},{2,6},{6,2},{3,7},{7,3},{8,12},{12,8},{9,1... | collective-permute-start | bytes 2359304 | tf_op jit(solution)/shard_map/ppermute | solution.py:627
  396.6 27.6 %collective-permute-start.50 = (bf16[256,1536]{1,0:T(8,128)(2,1)S(1)}, bf16[256,1536]{1,0:T(8,128)(2,1)S(1)}, u32[]{:S(2)}, u32[]{:S(2)}) collective-permute-start(bf16[256,1536]{1,0:T(8,128)(2,1)S(1)} %add_convert_fusion.6), channel_id=1, source_target_pairs={{0,8},{8,0},{1,9},{9,1},{2,10},{10,2},{3,11},{11,3},{4,12},{12,4},... | collective-permute-start | bytes 2359304 | tf_op jit(solution)/shard_map/ppermute | solution.py:627
  441.8 28.7 %collective-permute-start.53 = (bf16[2,192,768]{2,1,0:T(8,128)(2,1)}, bf16[2,192,768]{2,1,0:T(8,128)(2,1)}, u32[]{:S(2)}, u32[]{:S(2)}) collective-permute-start(bf16[2,192,768]{2,1,0:T(8,128)(2,1)} %get-tuple-element.404), channel_id=1, source_target_pairs={{0,16},{16,0},{1,17},{17,1},{2,18},{18,2},{3,19},{19,3},{4,20},{20... | collective-permute-start | bytes 1769480 | tf_op jit(solution)/shard_map/ppermute | solution.py:627
  443.3 44.1 %collective-permute-start.55 = (bf16[3,768,256]{2,1,0:T(8,128)(2,1)}, bf16[3,768,256]{2,1,0:T(8,128)(2,1)}, u32[]{:S(2)}, u32[]{:S(2)}) collective-permute-start(bf16[3,768,256]{2,1,0:T(8,128)(2,1)} %add_convert_fusion.2), channel_id=1, source_target_pairs={{0,1},{1,0},{2,3},{3,2},{4,5},{5,4},{6,7},{7,6},{8,9},{9,8},{10,11... | collective-permute-start | bytes 3538952 | tf_op jit(solution)/shard_map/ppermute | solution.py:631
  443.3 50.7 %collective-permute-start.56 = (bf16[3,768,256]{2,1,0:T(8,128)(2,1)}, bf16[3,768,256]{2,1,0:T(8,128)(2,1)}, u32[]{:S(2)}, u32[]{:S(2)}) collective-permute-start(bf16[3,768,256]{2,1,0:T(8,128)(2,1)} %get-tuple-element.411), channel_id=1, source_target_pairs={{0,16},{16,0},{1,17},{17,1},{2,18},{18,2},{3,19},{19,3},{4,20},{20... | collective-permute-start | bytes 3538952 | tf_op jit(solution)/shard_map/ppermute | solution.py:627
  443.8 43.6 %collective-permute-start.54 = (bf16[2,768,256]{2,1,0:T(8,128)(2,1)}, bf16[2,768,256]{2,1,0:T(8,128)(2,1)}, u32[]{:S(2)}, u32[]{:S(2)}) collective-permute-start(bf16[2,768,256]{2,1,0:T(8,128)(2,1)} %slice.92), channel_id=1, source_target_pairs={{0,3},{1,2},{2,1},{3,0},{4,7},{5,6},{6,5},{7,4},{8,11},{9,10},{10,... | collective-permute-start | bytes 2359304 | tf_op jit(solution)/shard_map/ppermute | solution.py:631
  500.2 20.6 %collective-permute-start.57 = (bf16[288,768]{1,0:T(8,128)(2,1)}, bf16[288,768]{1,0:T(8,128)(2,1)}, u32[]{:S(2)}, u32[]{:S(2)}) collective-permute-start(bf16[288,768]{1,0:T(8,128)(2,1)} %copy-done.79), channel_id=1, source_target_pairs={{0,1},{1,0},{2,3},{3,2},{4,5},{5,4},{6,7},{7,6},{8,9},{9,8},{10,11... | collective-permute-start | bytes 1327112 | tf_op jit(solution)/shard_map/ppermute | solution.py:631
  500.2 29.8 %collective-permute-start.58 = (bf16[288,768]{1,0:T(8,128)(2,1)}, bf16[288,768]{1,0:T(8,128)(2,1)S(1)}, u32[]{:S(2)}, u32[]{:S(2)}) collective-permute-start(bf16[288,768]{1,0:T(8,128)(2,1)} %copy-done.78), channel_id=1, source_target_pairs={{0,1},{1,0},{2,3},{3,2},{4,5},{5,4},{6,7},{7,6},{8,9},{9,8},{10,11... | collective-permute-start | bytes 1327112 | tf_op jit(solution)/shard_map/ppermute | solution.py:631
  504.2 25.7 %collective-permute-start.60 = (bf16[256,1536]{1,0:T(8,128)(2,1)S(1)}, bf16[256,1536]{1,0:T(8,128)(2,1)S(1)}, u32[]{:S(2)}, u32[]{:S(2)}) collective-permute-start(bf16[256,1536]{1,0:T(8,128)(2,1)S(1)} %fusion.11), channel_id=1, source_target_pairs={{0,8},{8,0},{1,9},{9,1},{2,10},{10,2},{3,11},{11,3},{4,12},{12,4},... | collective-permute-start | bytes 2359304 | tf_op jit(solution)/shard_map/ppermute | solution.py:627
  (167 other events, 1946.1 us)

commit v2 on v1

--- a/solution.py
+++ b/solution.py
@@ -868,13 +868,15 @@
         gone = [(kept, swap(piece, "y")) for kept, piece in zip(qkv_grads[:2], qkv_grads[2:])]
     else:
         gone = [(lax.psum_scatter(piece, "y", scatter_dimension=2, tiled=True),) for piece in qkv_grads]
-    own_came = crossed(feed_grads, 0)
+    own_came = swap(feed_grads[1][:2], "y") if parts == 2 else crossed(feed_grads, 0)
     gains = jnp.stack([gain_one[0], gain_two]).reshape(2, sequences, 2, 2, shard)
     sums = settle_attn(ids, gone, out_sums)
-    sums, feed_grads, onward, onward_down, feed_one, near, far, own_came, gains = fence(
-        (sums, feed_grads, onward, onward_down, feed_one, near, far, own_came, gains)
+    own_gone = feed_grads[1][2:]
+    sums, feed_grads, onward, onward_down, feed_one, near, far, own_came, own_gone, gains = fence(
+        (sums, feed_grads, onward, onward_down, feed_one, near, far, own_came, own_gone, gains)
     )
     onto_three = (sums[3].astype(F32) + sent(sums[2], "z", 1).astype(F32)).astype(BF16)
+    own_came = jnp.concatenate([own_came, swap(own_gone, "y")]) if parts == 2 else own_came
     onto_one = sent(sums[1], "z", 1)
     onward_down = sent(onward_down, "z", 3)
     total = near.astype(F32) + swap(far, "c").astype(F32)

time: 576 us -> 573 us (level)
  waiting for transfers between devices: 263 us -> 255 us
    ppermute x20, waiting for transfers between devices: 62.9 us -> 52 us  [sent(): lax.ppermute(value, axis, [(i, i ^ bits) for i in range(lax.axis_size(axi...]
    ppermute x51 -> x52, waiting for transfers between devices: 178 us -> 181 us  [swap(): return lax.ppermute(value, axis, [(0, 1), (1, 0)])]
    ppermute x51 -> x52, starting transfers between devices: 32.9 us -> 34.4 us  [swap(): return lax.ppermute(value, axis, [(0, 1), (1, 0)])]
    unnamed x241 -> x245, local copies, waits for them, and re-layouts: 37.8 us -> 38.6 us
  transfers between devices with their start and end apart: 79 -> 80, of which waited for: 40 -> 41; matrix products, arithmetic and copies ran while one was open for 6% -> 6% of each run, Pallas kernels for 19% -> 19%
where the time goes in v2:
time: 573 us; the launch traced here: 565 us
  waiting for transfers between devices  255 us (45%)
  Pallas kernels  134 us (23%)
  starting transfers between devices  86.1 us (15%)
  local copies, waits for them, and re-layouts  46.5 us (8%)
  other arithmetic  41.2 us (7%)
    ppermute x52, waiting for transfers between devices, swap(): return lax.ppermute(value, axis, [(0, 1), (1, 0)])  181 us
    pallas_call x18, Pallas kernels, run(): pl.pallas_call(kernel, out_shape=[shape(*o) if isinstance(o[0], tuple) el...  80.3 us
    ppermute x20, waiting for transfers between devices, sent(): lax.ppermute(value, axis, [(i, i ^ bits) for i in range(lax.axis_size(axi...  52 us
    unnamed x245, local copies, waits for them, and re-layouts  38.6 us
    pallas_call x1, Pallas kernels, attend_back(): pl.pallas_call(functools.partial(attend_back_kernel, block=block, tile=ti...  35 us
    ppermute x52, starting transfers between devices, swap(): return lax.ppermute(value, axis, [(0, 1), (1, 0)])  34.4 us
    ppermute x20, starting transfers between devices, sent(): lax.ppermute(value, axis, [(i, i ^ bits) for i in range(lax.axis_size(axi...  31.1 us
    pallas_call x1, Pallas kernels, attend(): pl.pallas_call(functools.partial(attend_kernel, block=block, tile=tile),...  18.7 us
  transfers between devices with their start and end apart: 80, of which 41 were waited for; matrix products, arithmetic and copies ran while one was open for 6% of the time, Pallas kernels for 19%

profile of v2, /device:TPU:0, one launch (start us, length us, event | category | flops | bytes accessed | tf_op | source)
XLA Modules:
  0.0 564.7 jit_solution(14629567843549875518)
XLA Ops:
  25.4 8.4 %collective-permute-done.4.refs_2_ = bf16[3,192,256]{2,1,0:T(8,128)(2,1)S(1)} collective-permute-done((bf16[3,192,256]{2,1,0:T(8,128)(2,1)S(1)}, bf16[3,192,256]{2,1,0:T(8,128)(2,1)S(1)}, u32[]{:S(2)}, u32[]{:S(2)}) %collective-permute-start.4) | collective-permute-done | bytes 294944 | tf_op jit(solution)/shard_map/ppermute | solution.py:627
  33.8 4.1 collective-permute-done.5.refs_3_
  38.5 4.1 collective-permute-done.7
  47.9 16.3 %collective-permute-done.13.refs_2_.refs_3_ = bf16[256,1536]{1,0:T(8,128)(2,1)S(1)} collective-permute-done((bf16[256,1536]{1,0:T(8,128)(2,1)S(1)}, bf16[256,1536]{1,0:T(8,128)(2,1)S(1)}, u32[]{:S(2)}, u32[]{:S(2)}) %collective-permute-start.13) | collective-permute-done | bytes 786464 | tf_op jit(solution)/shard_map/ppermute | solution.py:627
  71.4 8.6 %collective-permute-done.15.refs_9_.refs_5_.refs_10_ = bf16[288,768]{1,0:T(8,128)(2,1)S(1)} collective-permute-done((bf16[288,768]{1,0:T(8,128)(2,1)S(1)}, bf16[288,768]{1,0:T(8,128)(2,1)S(1)}, u32[]{:S(2)}, u32[]{:S(2)}) %collective-permute-start.15) | collective-permute-done | bytes 442400 | tf_op jit(solution)/shard_map/ppermute | solution.py:627
  80.0 5.1 project.1
  89.5 4.8 all-to-all-start
  96.4 17.3 %collective-permute-done.20.refs_2_.refs_6_ = bf16[256,1536]{1,0:T(8,128)(2,1)S(1)} collective-permute-done((bf16[256,1536]{1,0:T(8,128)(2,1)}, bf16[256,1536]{1,0:T(8,128)(2,1)S(1)}, u32[]{:S(2)}, u32[]{:S(2)}) %collective-permute-start.20) | collective-permute-done | bytes 786464 | tf_op jit(solution)/shard_map/ppermute | solution.py:627
  126.8 4.6 all-to-all-done.own
  135.9 18.7 %attend.1 = (bf16[4,256,384]{2,1,0:T(8,128)(2,1)S(1)}, bf16[4096,128]{1,0:T(8,128)(2,1)S(1)}, bf16[2,4096,128]{2,1,0:T(8,128)(2,1)S(1)}, bf16[4096,128]{1,0:T(8,128)(2,1)S(1)}, f32[8,4096]{1,0:T(8,128)S(1)}) custom-call(s32[3]{0:T(128)S(1)} %pad_add_fusion.ids, bf16[4,256,768]{2,1,0:T(8,128)(2,1)} %all-to-all-done.own, ...), custom_call_target="tpu_custom_call" | custom-call | flops 20999999488 | bytes 1 | tf_op jit(solution)/shard_map/attend/pallas_call | solution.py:112
  158.6 4.0 collective-permute-done.23.refs_7_
  164.6 4.4 all-to-all-start.1
  173.6 18.7 %collective-permute-done.27.refs_8_ = bf16[768,256]{1,0:T(8,128)(2,1)} collective-permute-done((bf16[768,256]{1,0:T(8,128)(2,1)}, bf16[768,256]{1,0:T(8,128)(2,1)}, u32[]{:S(2)}, u32[]{:S(2)}) %collective-permute-start.27) | collective-permute-done | bytes 393248 | tf_op jit(solution)/shard_map/ppermute | solution.py:631
  203.8 16.3 %collective-permute-done.29 = bf16[256,1536]{1,0:T(8,128)(2,1)S(1)} collective-permute-done((bf16[256,1536]{1,0:T(8,128)(2,1)S(1)}, bf16[256,1536]{1,0:T(8,128)(2,1)S(1)}, u32[]{:S(2)}, u32[]{:S(2)}) %collective-permute-start.29) | collective-permute-done | bytes 786464 | tf_op jit(solution)/shard_map/ppermute | solution.py:627
  222.8 17.7 %collective-permute-done.34.refs_0_.refs_2_ = bf16[256,1536]{1,0:T(8,128)(2,1)S(1)} collective-permute-done((bf16[256,1536]{1,0:T(8,128)(2,1)S(1)}, bf16[256,1536]{1,0:T(8,128)(2,1)S(1)}, u32[]{:S(2)}, u32[]{:S(2)}) %collective-permute-start.34) | collective-permute-done | bytes 786464 | tf_op jit(solution)/shard_map/ppermute | solution.py:627
  242.8 15.6 %feed.2 = (bf16[256,1536]{1,0:T(8,128)(2,1)S(1)}, bf16[256,1536]{1,0:T(8,128)(2,1)}, bf16[256,1536]{1,0:T(8,128)(2,1)S(1)}, bf16[256,1536]{1,0:T(8,128)(2,1)S(1)...) custom-call(s32[3]{0:T(128)S(1)} %pad_add_fusion.ids, ...), custom_call_target="tpu_custom_call" | custom-call | flops 18000001024 | bytes 1 | tf_op jit(solution)/shard_map/feed/pallas_call | solution.py:229
  263.6 15.2 %feed.3 = (bf16[256,1536]{1,0:T(8,128)(2,1)S(1)}, bf16[256,1536]{1,0:T(8,128)(2,1)S(1)}, bf16[256,1536]{1,0:T(8,128)(2,1)S(1)}, bf16[256,1536]{1,0:T(8,128)(2,1)...) custom-call(s32[3]{0:T(128)S(1)} %pad_add_fusion.ids, ...), custom_call_target="tpu_custom_call" | custom-call | flops 18000001024 | bytes 1 | tf_op jit(solution)/shard_map/feed/pallas_call | solution.py:229
  290.8 14.5 %feed_weights.1 = (bf16[3,768,256]{2,1,0:T(8,128)(2,1)S(1)}, bf16[3,768,256]{2,1,0:T(8,128)(2,1)}, bf16[3,768,256]{2,1,0:T(8,128)(2,1)}, bf16[3,768,256]{2,1,0:T...) custom-call(s32[3]{0:T(128)S(1)} %pad_add_fusion.ids, ...), custom_call_target="tpu_custom_call" | custom-call | flops 17000000512 | bytes 1 | tf_op jit(solution)/shard_map/feed_weights/pallas_call | solution.py:229
  305.3 4.1 collective-permute-done.40.refs_2_
  318.0 4.5 all-to-all-start.2
  322.6 15.5 %collective-permute-done.43 = bf16[3,768,256]{2,1,0:T(8,128)(2,1)} collective-permute-done((bf16[3,768,256]{2,1,0:T(8,128)(2,1)}, bf16[3,768,256]{2,1,0:T(8,128)(2,1)}, u32[]{:S(2)}, u32[]{:S(2)}) %collective-permute-start.43) | collective-permute-done | bytes 1179680 | tf_op jit(solution)/shard_map/ppermute | solution.py:627
  349.0 35.0 %attend_back.1 = (bf16[4,256,384]{2,1,0:T(8,128)(2,1)S(1)}, bf16[4096,128]{1,0:T(8,128)(2,1)S(1)}, bf16[4096,128]{1,0:T(8,128)(2,1)S(1)}) custom-call(s32[3]{0:T(128)S(1)} %pad_add_fusion.ids, bf16[4096,128]{1,0:T(8,128)(2,1)S(1)} %copy-done.88, bf16[2,4096,128]{2,1,0:T(8,128)(2,1)S(1)} %copy-done.86, bf16[4096,128]{1,0:T(8,128)(2,1)S(1)} %copy-done.90, ...), custom_call_target="tpu_custom_call" | custom-call | flops 38999998464 | bytes 1 | tf_op jit(solution)/shard_map/attend_back/pallas_call | solution.py:201
  389.9 4.6 all-to-all-start.3
  401.5 21.4 %collective-permute-done.51 = bf16[3,768,256]{2,1,0:T(8,128)(2,1)S(1)} collective-permute-done((bf16[3,768,256]{2,1,0:T(8,128)(2,1)}, bf16[3,768,256]{2,1,0:T(8,128)(2,1)S(1)}, u32[]{:S(2)}, u32[]{:S(2)}) %collective-permute-start.51) | collective-permute-done | bytes 1179680 | tf_op jit(solution)/shard_map/ppermute | solution.py:627
  435.4 5.8 %project_weights.1 = (bf16[1024,768]{1,0:T(8,128)(2,1)S(1)}, bf16[2,192,768]{2,1,0:T(8,128)(2,1)S(1)}, bf16[2,192,768]{2,1,0:T(8,128)(2,1)S(1)}, bf16[2,192,768]{2,1,0:T(8,128)(2,1)}, bf16[2,192,768]{2,1,0:T(8,128)(2,1)}) custom-call(s32[3]{0:T(128)S(1)} %pad_add_fusion.ids, bf16[4,256,768]{2,1,0:T(8,128)(2,1)} %all-to-all-done.3.refs_0_, ...), custom_call_target="tpu_custom_call" | custom-call | flops 99999997952 | bytes 1 | tf_op jit(solution)/shard_map/project_weights/pallas_call | solution.py:229
  454.1 4.6 collective-permute-done.52.refs_1_
  458.7 12.6 %collective-permute-done.53.refs_3_ = bf16[2,192,768]{2,1,0:T(8,128)(2,1)} collective-permute-done((bf16[2,192,768]{2,1,0:T(8,128)(2,1)}, bf16[2,192,768]{2,1,0:T(8,128)(2,1)}, u32[]{:S(2)}, u32[]{:S(2)}) %collective-permute-start.53) | collective-permute-done | bytes 589856 | tf_op jit(solution)/shard_map/ppermute | solution.py:627
  478.2 8.3 %collective-permute-done.56 = bf16[2,768,256]{2,1,0:T(8,128)(2,1)} collective-permute-done((bf16[2,768,256]{2,1,0:T(8,128)(2,1)}, bf16[2,768,256]{2,1,0:T(8,128)(2,1)}, u32[]{:S(2)}, u32[]{:S(2)}) %collective-permute-start.56) | collective-permute-done | bytes 786464 | tf_op jit(solution)/shard_map/ppermute | solution.py:627
  511.7 5.7 %collective-permute-done.57 = bf16[288,768]{1,0:T(8,128)(2,1)} collective-permute-done((bf16[288,768]{1,0:T(8,128)(2,1)}, bf16[288,768]{1,0:T(8,128)(2,1)}, u32[]{:S(2)}, u32[]{:S(2)}) %collective-permute-start.57) | collective-permute-done | bytes 442400 | tf_op jit(solution)/shard_map/ppermute | solution.py:631
  518.6 7.7 %collective-permute-done.58.one = bf16[288,768]{1,0:T(8,128)(2,1)S(1)} collective-permute-done((bf16[288,768]{1,0:T(8,128)(2,1)}, bf16[288,768]{1,0:T(8,128)(2,1)S(1)}, u32[]{:S(2)}, u32[]{:S(2)}) %collective-permute-start.58) | collective-permute-done | bytes 442400 | tf_op jit(solution)/shard_map/ppermute | solution.py:631
  539.5 5.5 collective-permute-done.68.refs_3_
  548.5 7.9 %collective-permute-start.73 = (f32[387]{0:T(512)S(1)}, f32[387]{0:T(512)S(1)}, u32[]{:S(2)}, u32[]{:S(2)}) collective-permute-start(f32[387]{0:T(512)S(1)} %constant_dynamic-update-slice_fusion), channel_id=1, source_target_pairs={{0,1},{1,0},{2,3},{3,2},{4,5},{5,4},{6,7},{7,6},{8,9},{9,8},{10,11... | collective-permute-start | bytes 4652 | tf_op jit(solution)/shard_map/ppermute | solution.py:631
  (469 shorter events, 220.9 us)
Async XLA Ops:
  22.4 20.2 %collective-permute-start.7 = (bf16[288,768]{1,0:T(8,128)(2,1)S(1)}, bf16[288,768]{1,0:T(8,128)(2,1)S(1)}, u32[]{:S(2)}, u32[]{:S(2)}) collective-permute-start(bf16[288,768]{1,0:T(8,128)(2,1)S(1)} %join_attn.1.refs_4_.refs_0_.refs_5_), channel_id=1, source_target_pairs={{0,1},{1,0},{2,3},{3,2},{4,5},{5,4},{6,7},{7,6},{8,9},{9,8},{10,11... | collective-permute-start | bytes 1327112 | tf_op jit(solution)/shard_map/ppermute | solution.py:631
  22.4 20.2 %collective-permute-start.8 = (bf16[288,768]{1,0:T(8,128)(2,1)S(1)}, bf16[288,768]{1,0:T(8,128)(2,1)S(1)}, u32[]{:S(2)}, u32[]{:S(2)}) collective-permute-start(bf16[288,768]{1,0:T(8,128)(2,1)S(1)} %join_attn.1.refs_4_.refs_0_.refs_5_), channel_id=1, source_target_pairs={{0,16},{16,0},{1,17},{17,1},{2,18},{18,2},{3,19},{19,3},{4,20},{20... | collective-permute-start | bytes 1327112 | tf_op jit(solution)/shard_map/ppermute | solution.py:627
  42.7 24.0 %collective-permute-start.10 = (bf16[2,288,768]{2,1,0:T(8,128)(2,1)S(1)}, bf16[2,288,768]{2,1,0:T(8,128)(2,1)S(1)}, u32[]{:S(2)}, u32[]{:S(2)}) collective-permute-start(bf16[2,288,768]{2,1,0:T(8,128)(2,1)S(1)} %pad_maximum_fusion.1.refs_6_.refs_2_.refs_7_), channel_id=1, source_target_pairs={{0,16},{16,0},{1,17},{17,1},{2,18},{18,2},{3,19},{19,3},{4,20},{20... | collective-permute-start | bytes 2654216 | tf_op jit(solution)/shard_map/ppermute | solution.py:627
  44.2 20.0 %collective-permute-start.13 = (bf16[256,1536]{1,0:T(8,128)(2,1)S(1)}, bf16[256,1536]{1,0:T(8,128)(2,1)S(1)}, u32[]{:S(2)}, u32[]{:S(2)}) collective-permute-start(bf16[256,1536]{1,0:T(8,128)(2,1)S(1)} %fusion.1.refs_0_.refs_1_), channel_id=1, source_target_pairs={{0,8},{8,0},{1,9},{9,1},{2,10},{10,2},{3,11},{11,3},{4,12},{12,4},... | collective-permute-start | bytes 2359304 | tf_op jit(solution)/shard_map/ppermute | solution.py:627
  45.7 20.9 %collective-permute-start.9 = (bf16[288,768]{1,0:T(8,128)(2,1)S(1)}, bf16[288,768]{1,0:T(8,128)(2,1)S(1)}, u32[]{:S(2)}, u32[]{:S(2)}) collective-permute-start(bf16[288,768]{1,0:T(8,128)(2,1)S(1)} %collective-permute-done.6), channel_id=1, source_target_pairs={{0,1},{1,0},{2,3},{3,2},{4,5},{5,4},{6,7},{7,6},{8,9},{9,8},{10,11... | collective-permute-start | bytes 1327112 | tf_op jit(solution)/shard_map/ppermute | solution.py:631
  68.6 20.8 %collective-permute-start.17 = (bf16[768,256]{1,0:T(8,128)(2,1)S(1)}, bf16[768,256]{1,0:T(8,128)(2,1)}, u32[]{:S(2)}, u32[]{:S(2)}) collective-permute-start(bf16[768,256]{1,0:T(8,128)(2,1)S(1)} %get-tuple-element.481), channel_id=1, source_target_pairs={{0,3},{1,2},{2,1},{3,0},{4,7},{5,6},{6,5},{7,4},{8,11},{9,10},{10,... | collective-permute-start | bytes 1179656 | tf_op jit(solution)/shard_map/ppermute | solution.py:631
  89.5 41.9 %all-to-all-start = ((bf16[4,256,768]{2,1,0:T(8,128)(2,1)}), bf16[4,256,768]{2,1,0:T(8,128)(2,1)}, u32[]{:S(2)}, u32[]{:S(2)}) async-start(bf16[4,256,768]{2,1,0:T(8,128)(2,1)} %copy-done), calls=%async_computation | async-start | bytes 3145728 | tf_op jit(solution)/shard_map/all_to_all | solution.py:652
  94.9 30.0 %collective-permute-start.18 = (bf16[3,768,256]{2,1,0:T(8,128)(2,1)S(1)}, bf16[3,768,256]{2,1,0:T(8,128)(2,1)S(1)}, u32[]{:S(2)}, u32[]{:S(2)}) collective-permute-start(bf16[3,768,256]{2,1,0:T(8,128)(2,1)S(1)} %join_ffn.1.refs_4_), channel_id=1, source_target_pairs={{0,16},{16,0},{1,17},{17,1},{2,18},{18,2},{3,19},{19,3},{4,20},{20... | collective-permute-start | bytes 3538952 | tf_op jit(solution)/shard_map/ppermute | solution.py:627
  96.4 27.6 %collective-permute-start.19 = (bf16[256,1536]{1,0:T(8,128)(2,1)}, bf16[256,1536]{1,0:T(8,128)(2,1)S(1)}, u32[]{:S(2)}, u32[]{:S(2)}) collective-permute-start(bf16[256,1536]{1,0:T(8,128)(2,1)} %refs_4_), channel_id=1, source_target_pairs={{0,4},{4,0},{1,5},{5,1},{2,6},{6,2},{3,7},{7,3},{8,12},{12,8},{9,1... | collective-permute-start | bytes 2359304 | tf_op jit(solution)/shard_map/ppermute | solution.py:627
  132.9 29.8 %collective-permute-start.25 = (bf16[3,768,256]{2,1,0:T(8,128)(2,1)S(1)}, bf16[3,768,256]{2,1,0:T(8,128)(2,1)S(1)}, u32[]{:S(2)}, u32[]{:S(2)}) collective-permute-start(bf16[3,768,256]{2,1,0:T(8,128)(2,1)S(1)} %copy-done.20), channel_id=1, source_target_pairs={{0,16},{16,0},{1,17},{17,1},{2,18},{18,2},{3,19},{19,3},{4,20},{20... | collective-permute-start | bytes 3538952 | tf_op jit(solution)/shard_map/ppermute | solution.py:627
  134.4 28.2 %collective-permute-start.24 = (bf16[2,768,256]{2,1,0:T(8,128)(2,1)}, bf16[2,768,256]{2,1,0:T(8,128)(2,1)S(1)}, u32[]{:S(2)}, u32[]{:S(2)}) collective-permute-start(bf16[2,768,256]{2,1,0:T(8,128)(2,1)} %pad_maximum_fusion.2), channel_id=1, source_target_pairs={{0,1},{1,0},{2,3},{3,2},{4,5},{5,4},{6,7},{7,6},{8,9},{9,8},{10,11... | collective-permute-start | bytes 2359304 | tf_op jit(solution)/shard_map/ppermute | solution.py:631
  134.5 28.1 %collective-permute-start.23 = (bf16[768,256]{1,0:T(8,128)(2,1)S(1)}, bf16[768,256]{1,0:T(8,128)(2,1)}, u32[]{:S(2)}, u32[]{:S(2)}) collective-permute-start(bf16[768,256]{1,0:T(8,128)(2,1)S(1)} %copy-done.113), channel_id=1, source_target_pairs={{0,3},{1,2},{2,1},{3,0},{4,7},{5,6},{6,5},{7,4},{8,11},{9,10},{10,... | collective-permute-start | bytes 1179656 | tf_op jit(solution)/shard_map/ppermute | solution.py:631
  164.6 28.7 %all-to-all-start.1 = ((bf16[4,256,384]{2,1,0:T(8,128)(2,1)}), bf16[4,256,384]{2,1,0:T(8,128)(2,1)}, u32[]{:S(2)}, u32[]{:S(2)}) async-start(bf16[4,256,384]{2,1,0:T(8,128)(2,1)} %copy-done.35), calls=%async_computation.1 | async-start | bytes 1572864 | tf_op jit(solution)/shard_map/all_to_all | solution.py:652
  168.9 23.4 %collective-permute-start.26 = (bf16[2,768,256]{2,1,0:T(8,128)(2,1)}, bf16[2,768,256]{2,1,0:T(8,128)(2,1)S(1)}, u32[]{:S(2)}, u32[]{:S(2)}) collective-permute-start(bf16[2,768,256]{2,1,0:T(8,128)(2,1)} %copy-done.74), channel_id=1, source_target_pairs={{0,16},{16,0},{1,17},{17,1},{2,18},{18,2},{3,19},{19,3},{4,20},{20... | collective-permute-start | bytes 2359304 | tf_op jit(solution)/shard_map/ppermute | solution.py:627
  169.5 22.8 %collective-permute-start.27 = (bf16[768,256]{1,0:T(8,128)(2,1)}, bf16[768,256]{1,0:T(8,128)(2,1)}, u32[]{:S(2)}, u32[]{:S(2)}) collective-permute-start(bf16[768,256]{1,0:T(8,128)(2,1)} %get-tuple-element.290), channel_id=1, source_target_pairs={{0,1},{1,0},{2,3},{3,2},{4,5},{5,4},{6,7},{7,6},{8,9},{9,8},{10,11... | collective-permute-start | bytes 1179656 | tf_op jit(solution)/shard_map/ppermute | solution.py:631
  201.4 20.2 %collective-permute-start.30 = (bf16[2,768,256]{2,1,0:T(8,128)(2,1)S(1)}, bf16[2,768,256]{2,1,0:T(8,128)(2,1)S(1)}, u32[]{:S(2)}, u32[]{:S(2)}) collective-permute-start(bf16[2,768,256]{2,1,0:T(8,128)(2,1)S(1)} %copy-done.110), channel_id=1, source_target_pairs={{0,1},{1,0},{2,3},{3,2},{4,5},{5,4},{6,7},{7,6},{8,9},{9,8},{10,11... | collective-permute-start | bytes 2359304 | tf_op jit(solution)/shard_map/ppermute | solution.py:631
  309.4 28.7 %collective-permute-start.43 = (bf16[3,768,256]{2,1,0:T(8,128)(2,1)}, bf16[3,768,256]{2,1,0:T(8,128)(2,1)}, u32[]{:S(2)}, u32[]{:S(2)}) collective-permute-start(bf16[3,768,256]{2,1,0:T(8,128)(2,1)} %get-tuple-element.359), channel_id=1, source_target_pairs={{0,16},{16,0},{1,17},{17,1},{2,18},{18,2},{3,19},{19,3},{4,20},{20... | collective-permute-start | bytes 3538952 | tf_op jit(solution)/shard_map/ppermute | solution.py:627
  318.0 24.9 %all-to-all-start.2 = ((bf16[4,256,384]{2,1,0:T(8,128)(2,1)}), bf16[4,256,384]{2,1,0:T(8,128)(2,1)S(1)}, u32[]{:S(2)}, u32[]{:S(2)}) async-start(bf16[4,256,384]{2,1,0:T(8,128)(2,1)} %copy-done.36), calls=%async_computation.2 | async-start | bytes 1572864 | tf_op jit(solution)/shard_map/all_to_all | solution.py:652
  343.0 41.1 %collective-permute-start.46 = (bf16[4,96,768]{2,1,0:T(8,128)(2,1)}, bf16[4,96,768]{2,1,0:T(8,128)(2,1)S(1)}, u32[]{:S(2)}, u32[]{:S(2)}) collective-permute-start(bf16[4,96,768]{2,1,0:T(8,128)(2,1)} %copy-done.78), channel_id=1, source_target_pairs={{0,16},{16,0},{1,17},{17,1},{2,18},{18,2},{3,19},{19,3},{4,20},{20... | collective-permute-start | bytes 1769480 | tf_op jit(solution)/shard_map/ppermute | solution.py:627
  343.5 40.8 %collective-permute-start.44 = (bf16[3,768,256]{2,1,0:T(8,128)(2,1)}, bf16[3,768,256]{2,1,0:T(8,128)(2,1)S(1)}, u32[]{:S(2)}, u32[]{:S(2)}) collective-permute-start(bf16[3,768,256]{2,1,0:T(8,128)(2,1)} %add_convert_fusion.5), channel_id=1, source_target_pairs={{0,1},{1,0},{2,3},{3,2},{4,5},{5,4},{6,7},{7,6},{8,9},{9,8},{10,11... | collective-permute-start | bytes 3538952 | tf_op jit(solution)/shard_map/ppermute | solution.py:631
  343.5 40.8 %collective-permute-start.45 = (bf16[3,768,256]{2,1,0:T(8,128)(2,1)}, bf16[3,768,256]{2,1,0:T(8,128)(2,1)S(1)}, u32[]{:S(2)}, u32[]{:S(2)}) collective-permute-start(bf16[3,768,256]{2,1,0:T(8,128)(2,1)} %get-tuple-element.373), channel_id=1, source_target_pairs={{0,16},{16,0},{1,17},{17,1},{2,18},{18,2},{3,19},{19,3},{4,20},{20... | collective-permute-start | bytes 3538952 | tf_op jit(solution)/shard_map/ppermute | solution.py:627
  389.9 42.1 %all-to-all-start.3 = ((bf16[4,256,768]{2,1,0:T(8,128)(2,1)}), bf16[4,256,768]{2,1,0:T(8,128)(2,1)}, u32[]{:S(2)}, u32[]{:S(2)}) async-start(bf16[4,256,768]{2,1,0:T(8,128)(2,1)} %pack.1), calls=%async_computation.3 | async-start | bytes 3145728 | tf_op jit(solution)/shard_map/all_to_all | solution.py:652
  394.6 28.3 %collective-permute-start.51 = (bf16[3,768,256]{2,1,0:T(8,128)(2,1)}, bf16[3,768,256]{2,1,0:T(8,128)(2,1)S(1)}, u32[]{:S(2)}, u32[]{:S(2)}) collective-permute-start(bf16[3,768,256]{2,1,0:T(8,128)(2,1)} %get-tuple-element.397), channel_id=1, source_target_pairs={{0,16},{16,0},{1,17},{17,1},{2,18},{18,2},{3,19},{19,3},{4,20},{20... | collective-permute-start | bytes 3538952 | tf_op jit(solution)/shard_map/ppermute | solution.py:627
  395.2 29.1 %collective-permute-start.48 = (bf16[256,1536]{1,0:T(8,128)(2,1)}, bf16[256,1536]{1,0:T(8,128)(2,1)S(1)}, u32[]{:S(2)}, u32[]{:S(2)}) collective-permute-start(bf16[256,1536]{1,0:T(8,128)(2,1)} %copy-done.73), channel_id=1, source_target_pairs={{0,4},{4,0},{1,5},{5,1},{2,6},{6,2},{3,7},{7,3},{8,12},{12,8},{9,1... | collective-permute-start | bytes 2359304 | tf_op jit(solution)/shard_map/ppermute | solution.py:627
  396.6 27.7 %collective-permute-start.50 = (bf16[256,1536]{1,0:T(8,128)(2,1)S(1)}, bf16[256,1536]{1,0:T(8,128)(2,1)S(1)}, u32[]{:S(2)}, u32[]{:S(2)}) collective-permute-start(bf16[256,1536]{1,0:T(8,128)(2,1)S(1)} %add_convert_fusion.6), channel_id=1, source_target_pairs={{0,8},{8,0},{1,9},{9,1},{2,10},{10,2},{3,11},{11,3},{4,12},{12,4},... | collective-permute-start | bytes 2359304 | tf_op jit(solution)/shard_map/ppermute | solution.py:627
  442.6 28.7 %collective-permute-start.53 = (bf16[2,192,768]{2,1,0:T(8,128)(2,1)}, bf16[2,192,768]{2,1,0:T(8,128)(2,1)}, u32[]{:S(2)}, u32[]{:S(2)}) collective-permute-start(bf16[2,192,768]{2,1,0:T(8,128)(2,1)} %get-tuple-element.405), channel_id=1, source_target_pairs={{0,16},{16,0},{1,17},{17,1},{2,18},{18,2},{3,19},{19,3},{4,20},{20... | collective-permute-start | bytes 1769480 | tf_op jit(solution)/shard_map/ppermute | solution.py:627
  445.1 41.4 %collective-permute-start.56 = (bf16[2,768,256]{2,1,0:T(8,128)(2,1)}, bf16[2,768,256]{2,1,0:T(8,128)(2,1)}, u32[]{:S(2)}, u32[]{:S(2)}) collective-permute-start(bf16[2,768,256]{2,1,0:T(8,128)(2,1)} %slice.84), channel_id=1, source_target_pairs={{0,16},{16,0},{1,17},{17,1},{2,18},{18,2},{3,19},{19,3},{4,20},{20... | collective-permute-start | bytes 2359304 | tf_op jit(solution)/shard_map/ppermute | solution.py:627
  445.6 43.8 %collective-permute-start.55 = (bf16[3,768,256]{2,1,0:T(8,128)(2,1)}, bf16[3,768,256]{2,1,0:T(8,128)(2,1)}, u32[]{:S(2)}, u32[]{:S(2)}) collective-permute-start(bf16[3,768,256]{2,1,0:T(8,128)(2,1)} %add_convert_fusion.2), channel_id=1, source_target_pairs={{0,1},{1,0},{2,3},{3,2},{4,5},{5,4},{6,7},{7,6},{8,9},{9,8},{10,11... | collective-permute-start | bytes 3538952 | tf_op jit(solution)/shard_map/ppermute | solution.py:631
  445.6 43.8 %collective-permute-start.54 = (bf16[2,768,256]{2,1,0:T(8,128)(2,1)}, bf16[2,768,256]{2,1,0:T(8,128)(2,1)}, u32[]{:S(2)}, u32[]{:S(2)}) collective-permute-start(bf16[2,768,256]{2,1,0:T(8,128)(2,1)} %slice.100), channel_id=1, source_target_pairs={{0,3},{1,2},{2,1},{3,0},{4,7},{5,6},{6,5},{7,4},{8,11},{9,10},{10,... | collective-permute-start | bytes 2359304 | tf_op jit(solution)/shard_map/ppermute | solution.py:631
  496.8 20.6 %collective-permute-start.57 = (bf16[288,768]{1,0:T(8,128)(2,1)}, bf16[288,768]{1,0:T(8,128)(2,1)}, u32[]{:S(2)}, u32[]{:S(2)}) collective-permute-start(bf16[288,768]{1,0:T(8,128)(2,1)} %copy-done.80), channel_id=1, source_target_pairs={{0,1},{1,0},{2,3},{3,2},{4,5},{5,4},{6,7},{7,6},{8,9},{9,8},{10,11... | collective-permute-start | bytes 1327112 | tf_op jit(solution)/shard_map/ppermute | solution.py:631
  496.8 29.5 %collective-permute-start.58 = (bf16[288,768]{1,0:T(8,128)(2,1)}, bf16[288,768]{1,0:T(8,128)(2,1)S(1)}, u32[]{:S(2)}, u32[]{:S(2)}) collective-permute-start(bf16[288,768]{1,0:T(8,128)(2,1)} %copy-done.79), channel_id=1, source_target_pairs={{0,1},{1,0},{2,3},{3,2},{4,5},{5,4},{6,7},{7,6},{8,9},{9,8},{10,11... | collective-permute-start | bytes 1327112 | tf_op jit(solution)/shard_map/ppermute | solution.py:631
  500.8 25.4 %collective-permute-start.60 = (bf16[256,1536]{1,0:T(8,128)(2,1)S(1)}, bf16[256,1536]{1,0:T(8,128)(2,1)S(1)}, u32[]{:S(2)}, u32[]{:S(2)}) collective-permute-start(bf16[256,1536]{1,0:T(8,128)(2,1)S(1)} %fusion.11), channel_id=1, source_target_pairs={{0,8},{8,0},{1,9},{9,1},{2,10},{10,2},{3,11},{11,3},{4,12},{12,4},... | collective-permute-start | bytes 2359304 | tf_op jit(solution)/shard_map/ppermute | solution.py:627
  (170 other events, 1960.6 us)
